TPU v7x, 256 devices: a whole 4x4x8 slice. The times are simulated.
256 devices in a mesh: dp: 128 (over z, y, x), rep: 2 (over core).
Axes of the slice: x: 4, y: 4, z: 8, core: 2. Of those that a mesh axis runs over, the one named last changes fastest.
Arguments:
- activations: bfloat16 [188416, 4096], P(('dp', 'rep')), may hold values from -24 to 24
- out_grads: bfloat16 [188416, 512], P(('dp', 'rep')), may hold values from -6 to 6
- worker_error: bfloat16 [128, 4096, 512], P('dp', 'rep'), may hold values from -3 to 3
- momentum_codes: bfloat16 [4096, 512], P(('rep', 'dp')), may hold values from -1 to 1
- momentum_scale: float32 [4096], P(('rep', 'dp')), may hold values from 1 to 4
- server_error: float32 [4096, 512], P(('rep', 'dp')), may hold values from -0.6 to 0.6
- master_weight: float32 [4096, 512], P(('rep', 'dp')), may hold values from -4 to 4
- variance: float32 [4096, 512], P(('rep', 'dp')), may hold values from 0.001 to 1
Outputs:
- next_worker: bfloat16 [128, 4096, 512], P('dp', 'rep')
- next_codes: bfloat16 [4096, 512], P(('rep', 'dp'))
- next_scale: float32 [4096], P(('rep', 'dp'))
- next_server: float32 [4096, 512], P(('rep', 'dp'))
- next_master: float32 [4096, 512], P(('rep', 'dp'))
- weights_full: bfloat16 [4096, 512], P('rep')
All inputs are finite; a program needn't handle non-finite values. Where the computation divides by a largest or mean magnitude, that divisor is 1e-20 or more.
Results may differ from a plain program's by a relative error of at most 0.012.
Values may be sent and summed in bfloat16 or wider, within the bound.
A program may use at most 128 MiB of HBM per device.

v0:
```python
import math

import jax
import jax.numpy as jnp
from jax import lax
from jax.sharding import PartitionSpec as P

beta_one = 0.9
learn_rate = 0.02
grad_boost = 8.0
tiny_scale = 1e-06
tiny_root = 1e-08


def compress_rows(values):
    row_scale = jnp.mean(jnp.abs(values), axis=1) + tiny_scale
    row_codes = jnp.clip(values / row_scale[:, None], -1.0, 1.0).astype(jnp.bfloat16)
    return (row_codes, row_scale)


def body(
    activations,
    out_grads,
    worker_error,
    momentum_codes,
    momentum_scale,
    server_error,
    master_weight,
    variance,
):
    core_count = lax.axis_size("rep")
    owner_count = lax.axis_size("dp")
    grad_factor = grad_boost / math.sqrt(core_count * activations.shape[0])
    summed = lax.psum_scatter(
        jnp.dot(activations.T, out_grads, preferred_element_type=jnp.float32),
        "rep",
        scatter_dimension=0,
        tiled=True,
    )
    gradient = summed * grad_factor
    gathered_codes, gathered_scale = (
        lax.all_gather(momentum_codes, "dp", axis=0, tiled=True),
        lax.all_gather(momentum_scale.astype(jnp.bfloat16), "dp", axis=0, tiled=True).astype(
            momentum_scale.dtype
        ),
    )
    previous = gathered_codes.astype(jnp.float32) * gathered_scale[:, None]
    combined = (
        beta_one * previous + (1.0 - beta_one) * gradient + worker_error[0].astype(jnp.float32)
    )
    sent_codes, sent_scale = compress_rows(combined)
    decoded = sent_codes.astype(jnp.float32) * sent_scale[:, None]
    leftover = (combined - decoded).astype(jnp.bfloat16)[None]
    own_count = momentum_codes.shape[0]
    arrived_codes, arrived_scale = (
        lax.all_to_all(
            sent_codes.reshape(owner_count, own_count, -1),
            "dp",
            split_axis=0,
            concat_axis=0,
            tiled=True,
        ),
        lax.all_to_all(
            sent_scale.reshape(owner_count, own_count).astype(jnp.bfloat16),
            "dp",
            split_axis=0,
            concat_axis=0,
            tiled=True,
        ).astype(jnp.float32),
    )
    running = jnp.sum(arrived_codes.astype(jnp.float32) * arrived_scale[:, :, None], axis=0)
    average = running / owner_count
    shifted = average + server_error
    next_codes, next_scale = compress_rows(shifted)
    momentum = next_codes.astype(jnp.float32) * next_scale[:, None]
    next_server = shifted - momentum
    next_master = master_weight - learn_rate * momentum / (jnp.sqrt(variance) + tiny_root)
    weights_full = lax.all_gather(next_master.astype(jnp.bfloat16), "dp", axis=0, tiled=True)
    return (leftover, next_codes, next_scale, next_server, next_master, weights_full)


def solution(mesh):
    return jax.shard_map(
        body,
        mesh=mesh,
        in_specs=(
            P(("dp", "rep"), None),
            P(("dp", "rep"), None),
            P("dp", "rep", None),
            P(("rep", "dp"), None),
            P(("rep", "dp")),
            P(("rep", "dp"), None),
            P(("rep", "dp"), None),
            P(("rep", "dp"), None),
        ),
        out_specs=(
            P("dp", "rep", None),
            P(("rep", "dp"), None),
            P(("rep", "dp")),
            P(("rep", "dp"), None),
            P(("rep", "dp"), None),
            P("rep", None),
        ),
        check_vma=False,
    )
```

profile of v0, /device:TPU:2, one launch (start us, length us, event | category | flops | bytes accessed | tf_op | source)
XLA Modules:
  0.0 556.7 jit_solution(5998192434360401022)
XLA Ops:
  8.0 0.0 copy-start
  8.0 0.0 all-gather.3.cloned.1.call-start
  8.1 0.7 all-gather.3.cloned.1.call-update
  8.7 0.0 reduce-scatter.2.cloned.1.call-start
  8.8 0.3 copy-done
  9.1 8.6 %fusion.4 = f32[4096,512]{1,0:T(8,128)} fusion(bf16[736,4096]{1,0:T(8,128)(2,1)} %param.8, bf16[736,512]{1,0:T(8,128)(2,1)S(1)} %copy-done), kind=kOutput, calls=%fused_computation.16 | convolution fusion | flops 3087007744 | bytes 15171584 | tf_op jit(solution)/shard_map/dot_general | solution.py:35
  17.7 0.0 copy-start.7
  17.7 0.0 copy-start.8
  17.7 0.0 copy-start.1
  17.7 0.0 reduce-scatter.2.cloned.1.call-update
  17.7 0.6 copy-done.7
  18.4 0.0 copy-done.8
  18.4 0.6 dynamic-slice
  19.6 0.2 dynamic-update-slice
  19.9 348.5 %all-reduce = bf16[2048]{0:T(1024)(128)(2,1)S(1)} all-reduce(bf16[2048]{0:T(1024)(128)(2,1)S(1)} %dynamic-update-slice), channel_id=1, replica_groups=mesh['dp'=128,'rep'=2] {'dp'}, use_global_device_ids=true, to_apply=%add | all-reduce | flops 2048 | bytes 8192
  368.4 0.0 all-gather.3.cloned.1.call-done
  368.4 0.0 reduce-scatter.2.cloned.1.call-done
  368.4 0.0 copy-done.1
  368.4 5.0 abs_reduce_fusion
  373.4 0.7 convert_element_type.77
  374.1 11.9 %all-to-all-start.1 = ((bf16[128,1,16]{2,1,0:T(2,128)(2,1)}), bf16[128,1,16]{2,1,0:T(2,128)(2,1)S(1)}, u32[]{:S(2)}, u32[]{:S(2)}) async-start(bf16[128,1,16]{2,1,0:T(2,128)(2,1)} %convert_element_type.77), calls=%async_computation.2 | async-start | bytes 131072 | tf_op jit(solution)/shard_map/all_to_all | solution.py:63
  386.0 4.0 clamp_convert_fusion
  390.1 0.0 copy-start.2
  390.1 0.0 copy-start.4
  390.1 0.0 copy-start.5
  390.1 7.4 %all-to-all-done.1 = bf16[128,1,16]{2,1,0:T(2,128)(2,1)S(1)} async-done(((bf16[128,1,16]{2,1,0:T(2,128)(2,1)}), bf16[128,1,16]{2,1,0:T(2,128)(2,1)S(1)}, u32[]{:S(2)}, u32[]{:S(2)}) %all-to-all-start.1) | async-done | bytes 4128 | tf_op jit(solution)/shard_map/all_to_all | solution.py:63
  397.4 6.7 %all-to-all-start = ((bf16[128,16,512]{2,1,0:T(8,128)(2,1)}), bf16[128,16,512]{2,1,0:T(8,128)(2,1)S(1)}, u32[]{:S(2)}, u32[]{:S(2)}) async-start(bf16[128,16,512]{2,1,0:T(8,128)(2,1)} %bitcast.3), calls=%async_computation.1 | async-start | bytes 4194304 | tf_op jit(solution)/shard_map/all_to_all | solution.py:56
  404.1 0.0 all-gather.5.cloned.1.call-start
  404.2 0.1 convert_element_type.76
  404.3 31.1 %all-to-all-done = bf16[128,16,512]{2,1,0:T(8,128)(2,1)S(1)} async-done(((bf16[128,16,512]{2,1,0:T(8,128)(2,1)}), bf16[128,16,512]{2,1,0:T(8,128)(2,1)S(1)}, u32[]{:S(2)}, u32[]{:S(2)}) %all-to-all-start) | async-done | bytes 2097184 | tf_op jit(solution)/shard_map/all_to_all | solution.py:56
  435.4 0.5 multiply_reduce_fusion
  435.8 0.0 copy-done.2
  435.9 0.1 abs_reduce_fusion.1
  436.0 0.0 copy-done.4
  436.0 0.0 copy-done.5
  436.0 0.0 copy-start.6
  436.0 0.7 fusion.3
  436.7 0.0 copy-start.3
  436.7 0.0 all-gather.5.cloned.1.call-update
  436.7 0.7 fusion.1
  437.4 108.8 %all-gather.5.cloned.1.call-done = bf16[2048,512]{1,0:T(8,128)(2,1)} async-done(((bf16[16,512]{1,0:T(8,128)(2,1)}), bf16[2048,512]{1,0:T(8,128)(2,1)}) %all-gather.5.cloned.1.call-update) | async-done | bytes 2097168 | tf_op jit(solution)/shard_map/all_gather | solution.py:78
  546.2 3.0 copy.17
  549.2 0.0 copy-done.6
  549.2 0.0 copy-done.3
  (5 shorter events, 0.0 us)
Async XLA Ops:
  8.0 1.1 copy-start
  8.0 360.4 %all-gather.3.cloned.1.call-start = ((), (), s32[]{:S(2)}) async-start(), calls=%async_computation.3 | async-start | bytes 2113536 | tf_op jit(solution)/shard_map/all_gather | solution.py:42
  8.7 359.7 %reduce-scatter.2.cloned.1.call-start = ((), (), s32[]{:S(2)}) async-start(), calls=%async_computation.4 | async-start | bytes 12582912 | tf_op jit(solution)/shard_map/reduce_scatter | solution.py:34
  17.7 0.7 copy-start.7
  17.7 0.7 copy-start.8
  17.7 350.7 %copy-start.1 = (bf16[1,2048,512]{2,1,0:T(8,128)(2,1)S(1)}, bf16[1,2048,512]{2,1,0:T(8,128)(2,1)}, u32[]{:S(2)}) copy-start(bf16[1,2048,512]{2,1,0:T(8,128)(2,1)} %param.10) | copy-start | bytes 6291460
  374.1 23.3 %all-to-all-start.1 = ((bf16[128,1,16]{2,1,0:T(2,128)(2,1)}), bf16[128,1,16]{2,1,0:T(2,128)(2,1)S(1)}, u32[]{:S(2)}, u32[]{:S(2)}) async-start(bf16[128,1,16]{2,1,0:T(2,128)(2,1)} %convert_element_type.77), calls=%async_computation.2 | async-start | bytes 131072 | tf_op jit(solution)/shard_map/all_to_all | solution.py:63
  390.1 45.8 %copy-start.2 = (f32[16,512]{1,0:T(8,128)S(1)}, f32[16,512]{1,0:T(8,128)}, u32[]{:S(2)}) copy-start(f32[16,512]{1,0:T(8,128)} %param.13) | copy-start | bytes 98308
  390.1 45.9 %copy-start.4 = (f32[16,512]{1,0:T(8,128)S(1)}, f32[16,512]{1,0:T(8,128)}, u32[]{:S(2)}) copy-start(f32[16,512]{1,0:T(8,128)} %param.14) | copy-start | bytes 98308
  390.1 45.9 %copy-start.5 = (f32[16,512]{1,0:T(8,128)S(1)}, f32[16,512]{1,0:T(8,128)}, u32[]{:S(2)}) copy-start(f32[16,512]{1,0:T(8,128)} %param.15) | copy-start | bytes 98308
  397.4 37.9 %all-to-all-start = ((bf16[128,16,512]{2,1,0:T(8,128)(2,1)}), bf16[128,16,512]{2,1,0:T(8,128)(2,1)S(1)}, u32[]{:S(2)}, u32[]{:S(2)}) async-start(bf16[128,16,512]{2,1,0:T(8,128)(2,1)} %bitcast.3), calls=%async_computation.1 | async-start | bytes 4194304 | tf_op jit(solution)/shard_map/all_to_all | solution.py:56
  404.1 142.1 %all-gather.5.cloned.1.call-start = ((), (), s32[]{:S(2)}) async-start(), calls=%async_computation.5 | async-start | bytes 2113536 | tf_op jit(solution)/shard_map/all_gather | solution.py:78
  436.0 113.2 %copy-start.6 = (f32[16]{0:T(128)}, f32[16]{0:T(128)S(1)}, u32[]{:S(2)}) copy-start(f32[16]{0:T(128)S(1)} %multiply_add_fusion.2) | copy-start | bytes 196
  436.7 112.5 %copy-start.3 = (bf16[16,512]{1,0:T(8,128)(2,1)}, bf16[16,512]{1,0:T(8,128)(2,1)S(1)}, u32[]{:S(2)}) copy-start(bf16[16,512]{1,0:T(8,128)(2,1)S(1)} %get-tuple-element.22) | copy-start | bytes 49156
Sparse Core Ops, SparseCore 0:
  13.0 117.0 all-gather.2
  436.9 109.2 all-gather.4
Sparse Core Ops, SparseCore 1:
  17.8 25.1 reduce-scatter.1
where the time goes:
time: 557 us
  blocking collectives  348 us (62%)
  waiting for transfers between devices  148 us (27%)
  starting transfers between devices  18.7 us (3%)
  between operations  16.3 us (3%)
  other arithmetic  11.1 us (2%)
  matrix products  8.58 us (2%)
  local copies, waits for them, and re-layouts  5.61 us (1%)
    unnamed x1, blocking collectives  348 us
    all_gather x1, waiting for transfers between devices, body(): lax.all_gather(next_master.astype(jnp.bfloat16), 'dp', axis=0, tiled=True)  109 us
    all_to_all x1, waiting for transfers between devices, body(): lax.all_to_all(sent_codes.reshape(owner_count, own_count, -1), 'dp', spli...  31.1 us
    all_to_all x1, starting transfers between devices, body(): lax.all_to_all(sent_scale.reshape(owner_count, own_count).astype(jnp.bflo...  11.9 us
  transfers between devices with their start and end apart: 5, of which 3 were waited for; matrix products, arithmetic and copies ran while one was open for 3% of the time, Pallas kernels for 0%

commit v1 on v0

v1 whole, which is shorter than its diff:
```python
import math

import jax
import jax.numpy as jnp
from jax import lax
from jax.experimental import pallas as pl
from jax.experimental.pallas import tpu as pltpu
from jax.sharding import PartitionSpec as P

BF16 = jnp.bfloat16
F32 = jnp.float32
MESH = pl.DeviceIdType.MESH

NX, NY, NZ = 4, 4, 8
OWN = 16
LANES = 128
CHUNK = 256
HALF = 2048
WIDTH = 512
CHUNKS = HALF // CHUNK

beta_one = 0.9
learn_rate = 0.02
grad_boost = 8.0
tiny_scale = 1e-06
tiny_root = 1e-08


class Links:
    def __init__(self, send_sems, recv_sems, core):
        self.send_sems, self.recv_sems, self.core = send_sems, recv_sems, core
        self.used = 0
        self.open = []

    def sem(self):
        self.used += 1
        return self.used - 1

    def send(self, src, dst, sem, dp, rep=None):
        copy = pltpu.make_async_remote_copy(
            src_ref=src,
            dst_ref=dst,
            send_sem=self.send_sems.at[sem],
            recv_sem=self.recv_sems.at[sem],
            device_id={"dp": dp, "rep": self.core if rep is None else rep},
            device_id_type=MESH,
        )
        copy.start()
        self.open.append(copy)

    def arrived(self, dst, sem, dp):
        pltpu.make_async_remote_copy(
            src_ref=dst,
            dst_ref=dst,
            send_sem=self.send_sems.at[sem],
            recv_sem=self.recv_sems.at[sem],
            device_id={"dp": dp, "rep": self.core},
            device_id_type=MESH,
        ).wait_recv()

    def drain(self):
        for copy in self.open:
            copy.wait_send()
        self.open = []


class Ring:
    def __init__(self, links, size, me, dp_at):
        self.links, self.size, self.me, self.dp_at = links, size, me, dp_at
        self.reach = size // 2
        self.sems = {}
        for hop in range(1, self.reach + 1):
            for way in (1, -1):
                for half in (0, 1):
                    self.sems[way, hop, half] = links.sem()

    def at(self, offset):
        return lax.rem(self.me + (offset + self.size), self.size)

    def first(self, way):
        return 0 if way == 1 else 1

    def plan(self):
        for turn in (0, 1):
            for way in (1, -1):
                yield turn, way, self.first(way) if turn == 0 else 1 - self.first(way)

    def gather_hop(self, view, hop):
        for turn, way, half in self.plan():
            if hop == self.reach and turn == 1:
                continue
            part = view(self.at(-way * (hop - 1)), half)
            if hop > 1:
                self.links.arrived(part, self.sems[way, hop - 1, half], self.dp_at(self.at(-way)))
            self.links.send(part, part, self.sems[way, hop, half], self.dp_at(self.at(way)))

    def gather_end(self, view):
        for turn, way, half in self.plan():
            if turn == 1:
                hop = self.reach - 1
                part = view(self.at(-way * hop), half)
                self.links.arrived(part, self.sems[way, hop, half], self.dp_at(self.at(-way)))
        for turn, way, half in self.plan():
            if turn == 0:
                hop = self.reach
                part = view(self.at(-way * hop), half)
                self.links.arrived(part, self.sems[way, hop, half], self.dp_at(self.at(-way)))

    def reduce_begin(self, view, slot):
        for turn, way, half in self.plan():
            hop = 1 if turn == 0 else 2
            self.links.send(
                view(self.at(way * (self.reach - hop + 1)), half),
                slot(way, hop, half),
                self.sems[way, hop, half],
                self.dp_at(self.at(way)),
            )

    def reduce_hop(self, view, slot, hop):
        for turn, way, half in self.plan():
            if hop == 2 and turn == 1:
                continue
            got = slot(way, hop - 1, half)
            self.links.arrived(got, self.sems[way, hop - 1, half], self.dp_at(self.at(-way)))
            part = view(self.at(way * (self.reach - hop + 1)), half)
            part[...] = (part[...].astype(F32) + got[...].astype(F32)).astype(BF16)
            self.links.send(
                part, slot(way, hop, half), self.sems[way, hop, half], self.dp_at(self.at(way))
            )

    def reduce_end(self, slot):
        for turn, way, half in self.plan():
            self.links.arrived(
                slot(way, self.reach, half),
                self.sems[way, self.reach, half],
                self.dp_at(self.at(-way)),
            )


class Part:
    def __init__(self, links, sizes, place, dp_of):
        self.links = links
        self.n_last, self.n_mid, self.n_first = sizes
        self.last, self.mid, self.first = place
        self.dp_of = dp_of

    def dp_last(self, j):
        return self.dp_of(j, self.mid, self.first)

    def dp_mid(self, j):
        return self.dp_of(self.last, j, self.first)

    def dp_first(self, j):
        return self.dp_of(self.last, self.mid, j)

    def first_at(self, offset):
        return lax.rem(self.first + (offset + self.n_first), self.n_first)

    def last_view(self, buf):
        step = self.n_mid // 2
        return lambda j, half: buf.at[j, pl.ds(half * step, step)]

    def mid_view(self, buf):
        step = self.n_first // 2
        return lambda j, half: buf.at[self.last, j, pl.ds(half * step, step)]

    def gather_first(self, buf):
        self.first_sems = [self.links.sem() for _ in range(1, self.n_first)]
        mine = buf.at[self.last, self.mid, self.first]
        for k in range(1, self.n_first):
            self.links.send(mine, mine, self.first_sems[k - 1], self.dp_first(self.first_at(k)))

    def gather_mid(self, buf):
        for k in range(1, self.n_first):
            j = self.first_at(-k)
            self.links.arrived(
                buf.at[self.last, self.mid, j], self.first_sems[k - 1], self.dp_first(j)
            )
        self.ring = Ring(self.links, self.n_mid, self.mid, self.dp_mid)
        self.ring.gather_hop(self.mid_view(buf), 1)

    def gather_mid_relay(self, buf):
        self.ring.gather_hop(self.mid_view(buf), 2)

    def gather_last(self, buf):
        self.ring.gather_end(self.mid_view(buf))
        self.ring = Ring(self.links, self.n_last, self.last, self.dp_last)
        self.ring.gather_hop(self.last_view(buf), 1)

    def gather_last_relay(self, buf, hop):
        if hop <= self.ring.reach:
            self.ring.gather_hop(self.last_view(buf), hop)

    def gather_end(self, buf):
        self.ring.gather_end(self.last_view(buf))

    def reduce_last(self, dec, got):
        step = self.n_mid // 2
        self.got = lambda way, hop, half: got.at[
            0 if way == 1 else 1, hop - 1, pl.ds(half * step, step)
        ]
        self.ring = Ring(self.links, self.n_last, self.last, self.dp_last)
        self.ring.reduce_begin(self.last_view(dec), self.got)

    def reduce_last_relay(self, dec, hop):
        if hop <= self.ring.reach:
            self.ring.reduce_hop(self.last_view(dec), self.got, hop)

    def reduce_mid(self, dec, got, partial, got_mid):
        reach = self.ring.reach
        self.ring.reduce_end(self.got)
        for j in range(self.n_mid):
            total = dec[self.last, j].astype(F32)
            total += got[0, reach - 1, j].astype(F32) + got[1, reach - 1, j].astype(F32)
            partial[j] = total.astype(BF16)
        step = self.n_first // 2
        self.got_mid = lambda way, hop, half: got_mid.at[
            0 if way == 1 else 1, hop - 1, pl.ds(half * step, step)
        ]
        self.partial_view = lambda j, half: partial.at[j, pl.ds(half * step, step)]
        self.ring = Ring(self.links, self.n_mid, self.mid, self.dp_mid)
        self.ring.reduce_begin(self.partial_view, self.got_mid)

    def reduce_mid_relay(self):
        self.ring.reduce_hop(self.partial_view, self.got_mid, 2)

    def reduce_first(self, partial, got_mid, sums, got_first):
        self.ring.reduce_end(self.got_mid)
        sums[...] = partial[self.mid].astype(F32) + (
            got_mid[0, 1].astype(F32) + got_mid[1, 1].astype(F32)
        )
        self.first_sems = [self.links.sem() for _ in range(1, self.n_first)]
        for k in range(1, self.n_first):
            j = self.first_at(k)
            self.links.send(
                sums.at[j], got_first.at[k - 1], self.first_sems[k - 1], self.dp_first(j)
            )

    def reduce_end(self, sums, got_first):
        total = sums[self.first]
        for k in range(1, self.n_first):
            self.links.arrived(
                got_first.at[k - 1], self.first_sems[k - 1], self.dp_first(self.first_at(-k))
            )
        for k in range(1, self.n_first):
            total += got_first[k - 1]
        return total


def step_kernel(
    act, grads, werr, mcodes, mscale, serr, master, variance,
    left_out, codes_out, scale_out, server_out, master_out, weights_out,
    act_v, grads_v, werr_v, mcodes_v, serr_v, master_v, variance_v,
    left_v, codes_v, server_v, new_master_v,
    own_g, peer_tx, peer_rx,
    mom, mom_c, dec, dec_c, wts, wts_c,
    got, got_c, partial, partial_c, got_mid, got_mid_c, sums, sums_c, got_first, got_first_c,
    in_sems, act_sems, out_sems, peer_send, peer_recv, send_sems, recv_sems,
):
    dp = lax.axis_index("dp")
    core = lax.axis_index("rep")
    x = lax.rem(dp, NX)
    y = lax.rem(dp // NX, NY)
    z = dp // (NX * NY)
    other = 1 - core
    tokens = act.shape[0]
    factor = (1.0 - beta_one) * grad_boost / math.sqrt(2 * tokens)

    def load(k, src, dst):
        copy = pltpu.make_async_copy(src, dst, in_sems.at[k])
        copy.start()
        return copy

    load_codes = load(0, mcodes, mcodes_v)
    load_grads = load(1, grads, grads_v)

    def act_copy(k):
        base = jnp.where(k < CHUNKS, other * HALF, core * HALF)
        column = pl.multiple_of(base + lax.rem(k, CHUNKS) * CHUNK, CHUNK)
        return pltpu.make_async_copy(
            act.at[:, pl.ds(column, CHUNK)], act_v.at[k], act_sems.at[k]
        )

    @pl.loop(0, 2 * CHUNKS)
    def _(k):
        act_copy(k).start()

    load_werr = load(2, werr, werr_v)
    load_serr = load(3, serr, serr_v)
    load_master = load(4, master, master_v)
    load_variance = load(5, variance, variance_v)

    def dp_at(zz, yy, xx):
        return zz * (NX * NY) + yy * NX + xx

    barrier = pltpu.get_barrier_semaphore()
    peers = [(dp_at(lax.rem(z + k, NZ), y, x), core) for k in range(1, NZ)]
    peers += [(dp_at(z, y, lax.rem(x + k, NX)), core) for k in range(1, NX)]
    peers += [(dp_at(z, lax.rem(y + k, NY), x), core) for k in (1, NY - 1)]
    peers += [(dp, other)]
    for peer_dp, peer_core in peers:
        pl.semaphore_signal(
            barrier, inc=1, device_id={"dp": peer_dp, "rep": peer_core}, device_id_type=MESH
        )

    eye = lax.broadcasted_iota(jnp.int32, (OWN, OWN), 0) == lax.broadcasted_iota(
        jnp.int32, (OWN, OWN), 1
    )
    scale_col = jnp.sum(
        jnp.where(eye, jnp.broadcast_to(mscale[...], (OWN, OWN)), 0.0), axis=1, keepdims=True
    )
    load_codes.wait()
    previous = (mcodes_v[...].astype(F32) * scale_col).astype(BF16)

    links = Links(send_sems, recv_sems, core)
    def mixed(a, b):
        return a + core * (b - a)

    part_x = Part(links, (NX, NY, NZ), (x, y, z), lambda l, m, f: dp_at(f, m, l))
    part_y = Part(links, (NY, NX, NZ), (y, x, z), lambda l, m, f: dp_at(f, l, m))
    part_m = Part(
        links,
        (NX, NY, NZ),
        (mixed(x, y), mixed(y, x), z),
        lambda l, m, f: dp_at(f, mixed(m, l), mixed(l, m)),
    )
    part_z = Part(links, (NZ, NY, NX), (z, y, x), lambda l, m, f: dp_at(l, m, f))
    parts = [part_z, part_x, part_y, part_m]

    def bufs(three, one):
        return [one, three.at[0], three.at[1], three.at[2]]

    def columns(q):
        return slice(q * LANES, (q + 1) * LANES)

    quarter = [3, 0, 1, 2]

    moms = bufs(mom, mom_c)
    for part, buf, q in zip(parts, moms, quarter):
        buf[part.last, part.mid, part.first] = previous[:, columns(q)]
    pl.semaphore_wait(barrier, len(peers))

    for part, buf in zip(parts, moms):
        part.gather_first(buf)

    def product(k):
        act_copy(k).wait()
        return lax.dot_general(
            act_v[k], grads_v[...], (((0,), (0,)), ((), ())), preferred_element_type=F32
        )

    def chunk_rows(k):
        return pl.ds(pl.multiple_of(k * CHUNK, CHUNK), CHUNK)

    def peer_copy(k):
        rows = chunk_rows(k)
        return pltpu.make_async_remote_copy(
            src_ref=peer_tx.at[rows],
            dst_ref=peer_rx.at[rows],
            send_sem=peer_send.at[k],
            recv_sem=peer_recv.at[k],
            device_id={"dp": dp, "rep": other},
            device_id_type=MESH,
        )

    def for_other(lo, hi):
        @pl.loop(lo, hi)
        def _(k):
            peer_tx[chunk_rows(k)] = product(k).astype(BF16)
            peer_copy(k).start()

    def for_own(lo, hi):
        @pl.loop(lo, hi)
        def _(k):
            own_g[chunk_rows(k)] = product(k + CHUNKS)

    load_grads.wait()
    for_other(0, 4)
    for part, buf in zip(parts, moms):
        part.gather_mid(buf)
    for_other(4, 6)
    for part, buf in zip(parts, moms):
        part.gather_mid_relay(buf)
    for_other(6, 8)
    for part, buf in zip(parts, moms):
        part.gather_last(buf)
    for_own(0, 3)
    for part, buf in zip(parts, moms):
        part.gather_last_relay(buf, 2)
    for_own(3, 6)
    part_z.gather_last_relay(mom_c, 3)
    for_own(6, 8)
    part_z.gather_last_relay(mom_c, 4)

    load_werr.wait()

    @pl.loop(0, CHUNKS)
    def _(k):
        peer_copy(k).wait_recv()

    for part, buf in zip(parts, moms):
        part.gather_end(buf)

    def wide(q, value):
        return value[:, columns(q)]

    @pl.loop(0, NZ * NY)
    def _(t):
        zz = t // NY
        yy = lax.rem(t, NY)
        for xx in range(NX):
            rows = pl.ds(pl.multiple_of((t * NX + xx) * OWN, OWN), OWN)
            uu, vv = mixed(xx, yy), mixed(yy, xx)
            gradient = (own_g[rows, :] + peer_rx[rows, :].astype(F32)) * factor
            base = gradient + werr_v[rows, :].astype(F32)
            before = [mom[0, xx, yy, zz], mom[1, yy, xx, zz], mom[2, uu, vv, zz], mom_c[zz, yy, xx]]
            combined = [
                beta_one * before[q].astype(F32) + wide(q, base) for q in range(4)
            ]
            size = jnp.abs(combined[0]) + jnp.abs(combined[1])
            size += jnp.abs(combined[2]) + jnp.abs(combined[3])
            scale = jnp.sum(size, axis=1, keepdims=True) * (1.0 / WIDTH) + tiny_scale
            inverse = 1.0 / scale
            for q in range(4):
                codes = jnp.clip(combined[q] * inverse, -1.0, 1.0).astype(BF16)
                decoded = codes.astype(F32) * scale
                left_v[rows, columns(q)] = (combined[q] - decoded).astype(BF16)
                sent = decoded.astype(BF16)
                if q == 0:
                    dec[0, xx, yy, zz] = sent
                elif q == 1:
                    dec[1, yy, xx, zz] = sent
                elif q == 2:
                    dec[2, uu, vv, zz] = sent
                else:
                    dec_c[zz, yy, xx] = sent

    store_left = pltpu.make_async_copy(left_v, left_out, out_sems.at[0])
    store_left.start()

    decs, gots = bufs(dec, dec_c), bufs(got, got_c)
    halves, mids = bufs(partial, partial_c), bufs(got_mid, got_mid_c)
    totals, firsts = bufs(sums, sums_c), bufs(got_first, got_first_c)
    for part, d, g in zip(parts, decs, gots):
        part.reduce_last(d, g)
    for hop in (2, 3, 4):
        for part, d in zip(parts, decs):
            part.reduce_last_relay(d, hop)
    order = [1, 2, 3, 0]
    for i in order:
        parts[i].reduce_mid(decs[i], gots[i], halves[i], mids[i])
    for i in order:
        parts[i].reduce_mid_relay()
    for i in order:
        parts[i].reduce_first(halves[i], mids[i], totals[i], firsts[i])
    summed = [None] * 4
    for i in order:
        summed[quarter[i]] = parts[i].reduce_end(totals[i], firsts[i])

    load_serr.wait()
    load_master.wait()
    load_variance.wait()
    shifted = [summed[q] * (1.0 / (NX * NY * NZ)) + serr_v[:, columns(q)] for q in range(4)]
    size = jnp.abs(shifted[0]) + jnp.abs(shifted[1])
    size += jnp.abs(shifted[2]) + jnp.abs(shifted[3])
    scale = jnp.sum(size, axis=1, keepdims=True) * (1.0 / WIDTH) + tiny_scale
    wts_all = bufs(wts, wts_c)
    for i, part in enumerate(parts):
        q = quarter[i]
        codes = jnp.clip(shifted[q] / scale, -1.0, 1.0).astype(BF16)
        codes_v[:, columns(q)] = codes
        momentum = codes.astype(F32) * scale
        server_v[:, columns(q)] = shifted[q] - momentum
        new = master_v[:, columns(q)] - learn_rate * momentum / (
            jnp.sqrt(variance_v[:, columns(q)]) + tiny_root
        )
        new_master_v[:, columns(q)] = new
        wts_all[i][part.last, part.mid, part.first] = new.astype(BF16)
        part.gather_first(wts_all[i])
    scale_out[...] = jnp.sum(
        jnp.where(eye, jnp.broadcast_to(scale, (OWN, OWN)), 0.0), axis=0, keepdims=True
    )
    stores = [
        pltpu.make_async_copy(codes_v, codes_out, out_sems.at[1]),
        pltpu.make_async_copy(server_v, server_out, out_sems.at[2]),
        pltpu.make_async_copy(new_master_v, master_out, out_sems.at[3]),
    ]
    for copy in stores:
        copy.start()

    for part, buf in zip(parts, wts_all):
        part.gather_mid(buf)
    for part, buf in zip(parts, wts_all):
        part.gather_mid_relay(buf)
    for part, buf in zip(parts, wts_all):
        part.gather_last(buf)
    for hop in (2, 3, 4):
        for part, buf in zip(parts, wts_all):
            part.gather_last_relay(buf, hop)
    for i in order:
        parts[i].gather_end(wts_all[i])

    def place(k):
        xx, yy = lax.rem(k, NX), k // NX
        return [
            pltpu.make_async_copy(
                src, weights_out.at[:, yy, xx, :, pl.ds(q * LANES, LANES)], out_sems.at[4 + k * 3 + q]
            )
            for q, src in enumerate(
                [wts.at[0, xx, yy], wts.at[1, yy, xx], wts.at[2, mixed(xx, yy), mixed(yy, xx)]]
            )
        ]

    @pl.loop(0, NX * NY)
    def _(k):
        for copy in place(k):
            copy.start()

    whole = pltpu.make_async_copy(
        wts_c, weights_out.at[:, :, :, :, pl.ds(3 * LANES, LANES)], out_sems.at[4 + 3 * NX * NY]
    )
    whole.start()

    @pl.loop(0, NX * NY)
    def _(k):
        for copy in place(k):
            copy.wait()

    whole.wait()
    store_left.wait()
    for copy in stores:
        copy.wait()
    assert links.used == REMOTE_COPIES
    links.drain()

    @pl.loop(0, CHUNKS)
    def _(k):
        peer_copy(k).wait_send()


REMOTE_COPIES = 288


def body(act, grads, werr, mcodes, mscale, serr, master, variance):
    tokens = act.shape[0]
    any_spec = pl.BlockSpec(memory_space=pl.ANY)
    vmem_spec = pl.BlockSpec(memory_space=pltpu.VMEM)
    tile = (OWN, LANES)

    def vm(*shape, dtype=BF16):
        return pltpu.VMEM(shape, dtype)

    scratch = [
        vm(2 * CHUNKS, tokens, CHUNK),
        vm(tokens, WIDTH),
        vm(HALF, WIDTH),
        vm(OWN, WIDTH),
        vm(OWN, WIDTH, dtype=F32),
        vm(OWN, WIDTH, dtype=F32),
        vm(OWN, WIDTH, dtype=F32),
        vm(HALF, WIDTH),
        vm(OWN, WIDTH),
        vm(OWN, WIDTH, dtype=F32),
        vm(OWN, WIDTH, dtype=F32),
        vm(HALF, WIDTH, dtype=F32),
        vm(HALF, WIDTH),
        vm(HALF, WIDTH),
    ]
    for _ in range(3):
        scratch += [vm(3, 4, 4, NZ, *tile), vm(NZ, 4, 4, *tile)]
    scratch += [
        vm(3, 2, 2, 4, NZ, *tile),
        vm(2, 4, 4, 4, *tile),
        vm(3, 4, NZ, *tile),
        vm(4, 4, *tile),
        vm(3, 2, 2, NZ, *tile),
        vm(2, 2, 4, *tile),
        vm(3, NZ, *tile, dtype=F32),
        vm(4, *tile, dtype=F32),
        vm(3, NZ - 1, *tile, dtype=F32),
        vm(3, *tile, dtype=F32),
    ]
    dma = pltpu.SemaphoreType.DMA
    scratch += [
        dma((6,)),
        dma((2 * CHUNKS,)),
        dma((5 + 3 * NX * NY,)),
        dma((CHUNKS,)),
        dma((CHUNKS,)),
        dma((REMOTE_COPIES,)),
        dma((REMOTE_COPIES,)),
    ]
    shape = jax.ShapeDtypeStruct
    left, codes, scale, server, new_master, weights = pl.pallas_call(
        step_kernel,
        out_shape=[
            shape((HALF, WIDTH), BF16),
            shape((OWN, WIDTH), BF16),
            shape((1, OWN), F32),
            shape((OWN, WIDTH), F32),
            shape((OWN, WIDTH), F32),
            shape((NZ, NY, NX, OWN, WIDTH), BF16),
        ],
        in_specs=[any_spec] * 4 + [vmem_spec] + [any_spec] * 3,
        out_specs=[any_spec, any_spec, vmem_spec, any_spec, any_spec, any_spec],
        scratch_shapes=scratch,
        compiler_params=pltpu.CompilerParams(
            collective_id=0, has_side_effects=True, vmem_limit_bytes=48 * 1024 * 1024
        ),
        cost_estimate=pl.CostEstimate(
            flops=2 * tokens * 2 * HALF * WIDTH, bytes_accessed=14_000_000, transcendentals=0
        ),
        name="adam_step",
    )(act, grads, werr[0], mcodes, mscale.reshape(1, OWN), serr, master, variance)
    return (
        left[None],
        codes,
        scale.reshape(OWN),
        server,
        new_master,
        weights.reshape(HALF, WIDTH),
    )


def solution(mesh):
    return jax.shard_map(
        body,
        mesh=mesh,
        in_specs=(
            P(("dp", "rep"), None),
            P(("dp", "rep"), None),
            P("dp", "rep", None),
            P(("rep", "dp"), None),
            P(("rep", "dp")),
            P(("rep", "dp"), None),
            P(("rep", "dp"), None),
            P(("rep", "dp"), None),
        ),
        out_specs=(
            P("dp", "rep", None),
            P(("rep", "dp"), None),
            P(("rep", "dp")),
            P(("rep", "dp"), None),
            P(("rep", "dp"), None),
            P("rep", None),
        ),
        check_vma=False,
    )
```

time: 557 us -> 105 us (0.19)
  blocking collectives: 348 us -> 0 us
  waiting for transfers between devices: 148 us -> 0 us
  Pallas kernels: 0 us -> 93.2 us
  starting transfers between devices: 18.7 us -> 0 us
  between operations: 16.3 us -> 0.66 us
  other arithmetic: 11.1 us -> 0 us
  matrix products: 8.58 us -> 0 us
    unnamed x1 -> x0, blocking collectives: 348 us -> none
    all_gather x2 -> x0, waiting for transfers between devices: 109 us -> none  [the longest x1 109 us: body(): lax.all_gather(next_master.astype(jnp.bfloat16), 'dp', axis=0, tiled=True)]
    pallas_call x0 -> x1, Pallas kernels: none -> 93.2 us  [body(): pl.pallas_call(step_kernel, out_shape=[shape((HALF, WIDTH), BF16), shape(...]
    all_to_all x2 -> x0, waiting for transfers between devices: 38.5 us -> none  [the longest x1 31.1 us: body(): lax.all_to_all(sent_codes.reshape(owner_count, own_count, -1), 'dp', spli...]
    all_to_all x2 -> x0, starting transfers between devices: 18.6 us -> none  [the longest x1 11.9 us: body(): lax.all_to_all(sent_scale.reshape(owner_count, own_count).astype(jnp.bflo...]
    dot_general x1 -> x0, matrix products: 8.58 us -> none  [body(): jnp.dot(activations.T, out_grads, preferred_element_type=jnp.float32)]
  transfers between devices with their start and end apart: 5 -> 0, of which waited for: 3 -> 0; matrix products, arithmetic and copies ran while one was open for 3% -> 0% of each run, Pallas kernels for 0% -> 0%
where the time goes in v1:
time: 105 us; the launch traced here: 104 us
  Pallas kernels  93.2 us (89%)
  local copies, waits for them, and re-layouts  9.74 us (9%)
    pallas_call x1, Pallas kernels, body(): pl.pallas_call(step_kernel, out_shape=[shape((HALF, WIDTH), BF16), shape(...  93.2 us
    unnamed x18, local copies, waits for them, and re-layouts  9.74 us

profile of v1, /device:TPU:2, one launch (start us, length us, event | category | flops | bytes accessed | tf_op | source)
XLA Modules:
  0.0 103.6 jit_solution(14447127345895993537)
XLA Ops:
  0.6 0.0 copy-start
  0.6 1.1 %copy-done = bf16[736,512]{1,0:T(8,128)(2,1)S(1)} copy-done((bf16[736,512]{1,0:T(8,128)(2,1)S(1)}, bf16[736,512]{1,0:T(8,128)(2,1)}, u32[]{:S(2)}) %copy-start) | copy-done | bytes 753688
  1.8 0.0 copy-start.1
  1.8 0.8 copy-done.1
  2.5 0.0 copy-start.2
  2.5 0.8 copy-done.2
  3.3 0.0 copy-start.3
  3.3 0.8 copy-done.3
  4.0 0.0 copy-start.4
  4.0 0.7 copy-done.4
  4.8 0.0 copy-start.5
  4.8 0.7 copy-done.5
  5.4 93.2 %adam_step.1 = (bf16[2048,512]{1,0:T(8,128)(2,1)S(1)}, bf16[16,512]{1,0:T(8,128)(2,1)S(1)}, f32[1,16]{1,0:T(1,128)S(1)}, f32[16,512]{1,0:T(8,128)S(1)}, f32[16,5...) custom-call(bf16[736,4096]{1,0:T(8,128)(2,1)} %act.1, bf16[736,512]{1,0:T(8,128)(2,1)S(1)} %copy-done, ...), custom_call_target="tpu_custom_call" | custom-call | flops 3087007744 | bytes 14000000 | tf_op jit(solution)/shard_map/adam_step/pallas_call | solution.py:594
  98.6 1.3 %copy.20 = bf16[1,2048,512]{2,1,0:T(8,128)(2,1)} copy(bf16[1,2048,512]{2,1,0:T(8,128)(2,1)S(1)} %bitcast.6) | data formatting | bytes 4194304
  99.9 0.6 copy.21
  100.5 0.5 copy.22
  101.0 0.6 copy.23
  101.7 0.6 copy.24
  102.3 1.3 %copy.25 = bf16[2048,512]{1,0:T(8,128)(2,1)} copy(bf16[2048,512]{1,0:T(8,128)(2,1)S(1)} %bitcast.5) | data formatting | bytes 4194304
Async XLA Ops:
  0.6 1.1 %copy-start = (bf16[736,512]{1,0:T(8,128)(2,1)S(1)}, bf16[736,512]{1,0:T(8,128)(2,1)}, u32[]{:S(2)}) copy-start(bf16[736,512]{1,0:T(8,128)(2,1)} %grads.1) | copy-start | bytes 2260996
  1.8 0.8 copy-start.1
  2.5 0.8 copy-start.2
  3.3 0.8 copy-start.3
  4.0 0.7 copy-start.4
  4.8 0.7 copy-start.5

commit v2 on v0

v2 whole, which is shorter than its diff:
```python
import functools
import math

import jax
import jax.numpy as jnp
from jax import lax
from jax.experimental import pallas as pl
from jax.experimental.pallas import tpu as pltpu
from jax.sharding import PartitionSpec as P

BF16 = jnp.bfloat16
F32 = jnp.float32
MESH = pl.DeviceIdType.MESH

NX, NY, NZ = 4, 4, 8
RING = 4
OWN = 16
PART = 256
CHUNK = 256
HALF = 2048
WIDTH = 512
CHUNKS = HALF // CHUNK

beta_one = 0.9
learn_rate = 0.02
grad_boost = 8.0
tiny_scale = 1e-06
tiny_root = 1e-08


class Part:
    def __init__(self, column, p, q, dp_pq, core, send_sems, recv_sems):
        self.columns = slice(column, column + PART)
        self.p, self.q, self.dp_pq, self.core = p, q, dp_pq, core
        self.send_sems, self.recv_sems = send_sems, recv_sems

    def at_p(self, k):
        return lax.rem(self.p + (k + RING), RING)

    def at_q(self, k):
        return lax.rem(self.q + (k + RING), RING)

    def shard(self, buf, p, q, z):
        return buf.at[(p * RING + q) * NZ + z]

    def block(self, buf, p, q):
        return buf.at[pl.ds((p * RING + q) * NZ, NZ)]

    def half(self, buf, p, q, which):
        return buf.at[pl.ds((p * RING + q) * NZ + which * (NZ // 2), NZ // 2)]

    def send(self, src, dst, send, recv, dp):
        pltpu.make_async_remote_copy(
            src_ref=src,
            dst_ref=dst,
            send_sem=self.send_sems.at[send],
            recv_sem=self.recv_sems.at[recv],
            device_id={"dp": dp, "rep": self.core},
            device_id_type=MESH,
        ).start()

    def wait(self, like, recv):
        pltpu.make_async_copy(like, like, self.recv_sems.at[recv]).wait()

    def drain(self, like, send):
        pltpu.make_async_copy(like, like, self.send_sems.at[send]).wait()


G_FIRST, G_MID, G_LEFT, G_RIGHT, G_REST, G_COUNT = 0, 0, 4, 8, 12, 16
R_FIRST, R_MID, R_LEFT, R_RIGHT, R_REST, R_COUNT = 0, 1, 2, 6, 10, 14
G_SENDS, R_SENDS = 0, 1


class Gather:
    def __init__(self, part, buf, z, send, recv):
        self.part, self.buf, self.z, self.send_sem, self.recv = part, buf, z, send, recv

    def go(self, src, dst_recv, dp):
        self.part.send(src, src, self.send_sem, self.recv + dst_recv, dp)

    def first(self, dp_z):
        mine = self.part.shard(self.buf, self.part.p, self.part.q, self.z)
        for k in range(1, NZ):
            self.go(mine, G_FIRST, dp_z(lax.rem(self.z + k, NZ)))

    def first_here(self):
        self.part.wait(self.buf.at[pl.ds(0, NZ - 1)], self.recv + G_FIRST)

    def mid(self):
        part = self.part
        for k in (1, 3, 2):
            self.go(part.block(self.buf, part.p, part.q), G_MID + k, part.dp_pq(part.p, part.at_q(k)))

    def mid_here(self, k):
        part = self.part
        part.wait(part.block(self.buf, part.p, part.at_q(-k)), self.recv + G_MID + k)

    def last(self, row):
        part = self.part
        q = part.at_q(row)
        lower, upper = part.half(self.buf, part.p, q, 0), part.half(self.buf, part.p, q, 1)
        after = part.dp_pq(part.at_p(1), part.q)
        before = part.dp_pq(part.at_p(-1), part.q)
        self.go(lower, G_LEFT + row, after)
        self.go(upper, G_RIGHT + row, before)
        self.go(upper, G_REST + row, after)
        self.go(lower, G_REST + row, before)

    def relay(self, row):
        part = self.part
        q = part.at_q(row)
        lower = part.half(self.buf, part.at_p(-1), q, 0)
        part.wait(lower, self.recv + G_LEFT + row)
        self.go(lower, G_REST + row, part.dp_pq(part.at_p(1), part.q))
        upper = part.half(self.buf, part.at_p(1), q, 1)
        part.wait(upper, self.recv + G_RIGHT + row)
        self.go(upper, G_REST + row, part.dp_pq(part.at_p(-1), part.q))

    def row_here(self, row):
        self.part.wait(self.buf.at[pl.ds(0, 2 * NZ)], self.recv + G_REST + row)

    def drain(self):
        self.part.drain(self.buf.at[pl.ds(0, NX * NY * NZ - 1)], self.send_sem)


def gather_rest(gathers, before_blocks, own_block, near_rows, all_rows):
    for g in gathers:
        g.first_here()
    for g in gathers:
        g.mid()
        g.last(0)
    before_blocks()
    for k in (1, 3):
        for g in gathers:
            g.mid_here(k)
            g.last(RING - k)
    for g in gathers:
        g.relay(0)
    for g in gathers:
        g.mid_here(2)
        g.last(2)
    own_block()
    for row in (3, 1):
        for g in gathers:
            g.relay(row)
    for row in (0, 3, 1):
        for g in gathers:
            g.row_here(row)
    near_rows()
    for g in gathers:
        g.relay(2)
    for g in gathers:
        g.row_here(2)
    all_rows()


class Reduce:
    def __init__(self, part, dec, z, send, recv, near, far, partial, mids, sums, rounded, firsts):
        self.part, self.dec, self.z, self.send_sem, self.recv = part, dec, z, send, recv
        self.near, self.far, self.partial = near, far, partial
        self.mids, self.sums, self.rounded, self.firsts = mids, sums, rounded, firsts

    def go(self, src, dst, recv, dp):
        self.part.send(src, dst, self.send_sem, self.recv + recv, dp)

    def steps(self, row):
        part = self.part
        return (
            part.at_q(row),
            part.dp_pq(part.at_p(1), part.q),
            part.dp_pq(part.at_p(-1), part.q),
        )

    def half_of(self, row, way, which):
        return self.far.at[row, pl.ds(way * NZ + which * (NZ // 2), NZ // 2)]

    def last_far(self, row):
        part = self.part
        q, after, before = self.steps(row)
        opposite = part.at_p(2)
        self.go(part.half(self.dec, opposite, q, 0), self.near.at[row, 0], R_LEFT + row, after)
        self.go(part.half(self.dec, opposite, q, 1), self.near.at[row, 1], R_RIGHT + row, before)

    def last_own(self, row):
        part = self.part
        q, after, before = self.steps(row)
        self.go(part.half(self.dec, part.at_p(1), q, 1), self.half_of(row, 0, 1), R_REST + row, after)
        self.go(part.half(self.dec, part.at_p(-1), q, 0), self.half_of(row, 1, 0), R_REST + row, before)

    def last_relay(self, row):
        part = self.part
        q, after, before = self.steps(row)
        for way, sem, to, dp in ((0, R_LEFT, 1, after), (1, R_RIGHT, -1, before)):
            got = self.near.at[row, way]
            part.wait(got, self.recv + sem + row)
            mine = part.half(self.dec, part.at_p(to), q, way)
            mine[...] = (mine[...].astype(F32) + got[...].astype(F32)).astype(BF16)
            self.go(mine, self.half_of(row, way, way), R_REST + row, dp)

    def row_total(self, row):
        part = self.part
        part.wait(self.far.at[row], self.recv + R_REST + row)
        total = part.block(self.dec, part.p, part.at_q(row))[...].astype(F32)
        return total + (
            self.far[row, pl.ds(0, NZ)].astype(F32) + self.far[row, pl.ds(NZ, NZ)].astype(F32)
        )

    def mid(self, row):
        part = self.part
        self.partial[row] = self.row_total(row).astype(BF16)
        self.go(
            self.partial.at[row],
            self.mids.at[pl.ds((row - 1) * NZ, NZ)],
            R_MID,
            part.dp_pq(part.p, part.at_q(row)),
        )

    def mid_own(self):
        self.sums[...] = self.row_total(0)

    def first(self, dp_z):
        self.part.wait(self.mids, self.recv + R_MID)
        total = self.sums[...]
        for k in range(RING - 1):
            total += self.mids[pl.ds(k * NZ, NZ)].astype(F32)
        self.sums[...] = total
        self.rounded[...] = total.astype(BF16)
        for k in range(1, NZ):
            to = lax.rem(self.z + k, NZ)
            self.go(self.rounded.at[to], self.firsts.at[k - 1], R_FIRST, dp_z(to))

    def total(self):
        self.part.wait(self.firsts, self.recv + R_FIRST)
        total = self.sums[self.z]
        for k in range(NZ - 1):
            total += self.firsts[k].astype(F32)
        return total

    def drain(self):
        self.part.drain(self.dec.at[pl.ds(0, NX * NY * NZ - 1)], self.send_sem)


def step_kernel(
    act, grads, werr, mcodes, mscale, serr, master, variance,
    left_out, codes_out, scale_out, server_out, master_out, weights_out,
    act_v, grads_v, werr_v, mcodes_v, serr_v, master_v, variance_v,
    left_v, codes_v, server_v, new_master_v,
    own_g, peer_tx, peer_rx,
    mom, dec, wts, near, far, partial, mids, sums, rounded, firsts,
    in_sems, act_sems, out_sems, peer_send, peer_recv, send_sems, recv_sems,
):
    dp = lax.axis_index("dp")
    core = lax.axis_index("rep")
    x = lax.rem(dp, NX)
    y = lax.rem(dp // NX, NY)
    z = dp // (NX * NY)
    other = 1 - core
    tokens = act.shape[0]
    factor = (1.0 - beta_one) * grad_boost / math.sqrt(2 * tokens)

    def load(k, src, dst):
        copy = pltpu.make_async_copy(src, dst, in_sems.at[k])
        copy.start()
        return copy

    load_codes = load(0, mcodes, mcodes_v)

    def dp_at(zz, yy, xx):
        return zz * (NX * NY) + yy * NX + xx

    def dp_z(zz):
        return dp_at(zz, y, x)

    barrier = pltpu.get_barrier_semaphore()
    peers = [(dp_at(lax.rem(z + k, NZ), y, x), core) for k in range(1, NZ)]
    peers += [(dp_at(z, y, lax.rem(x + k, NX)), core) for k in range(1, NX)]
    peers += [(dp_at(z, lax.rem(y + k, NY), x), core) for k in range(1, NY)]
    peers += [(dp, other)]
    for peer_dp, peer_core in peers:
        pl.semaphore_signal(
            barrier, inc=1, device_id={"dp": peer_dp, "rep": peer_core}, device_id_type=MESH
        )

    load_grads = load(1, grads, grads_v)

    def act_copy(k):
        base = jnp.where(k < CHUNKS, other * HALF, core * HALF)
        column = pl.multiple_of(base + lax.rem(k, CHUNKS) * CHUNK, CHUNK)
        return pltpu.make_async_copy(
            act.at[:, pl.ds(column, CHUNK)], act_v.at[k], act_sems.at[k]
        )

    @pl.loop(0, 2 * CHUNKS)
    def _(k):
        act_copy(k).start()

    load_werr = load(2, werr, werr_v)
    load_serr = load(3, serr, serr_v)
    load_master = load(4, master, master_v)
    load_variance = load(5, variance, variance_v)

    eye = lax.broadcasted_iota(jnp.int32, (OWN, OWN), 0) == lax.broadcasted_iota(
        jnp.int32, (OWN, OWN), 1
    )
    scale_col = jnp.sum(
        jnp.where(eye, jnp.broadcast_to(mscale[...], (OWN, OWN)), 0.0), axis=1, keepdims=True
    )
    load_codes.wait()
    previous = (mcodes_v[...].astype(F32) * scale_col).astype(BF16)

    parts = [
        Part(0, x, y, lambda p, q: dp_at(z, q, p), core, send_sems, recv_sems),
        Part(PART, y, x, lambda p, q: dp_at(z, p, q), core, send_sems, recv_sems),
    ]
    gathers = []
    for i, part in enumerate(parts):
        part.shard(mom.at[i], part.p, part.q, z)[...] = previous[:, part.columns]
        gathers.append(Gather(part, mom.at[i], z, 3 * i, i * G_COUNT))
    pl.semaphore_wait(barrier, len(peers))
    for g in gathers:
        g.first(dp_z)

    def product(k):
        act_copy(k).wait()
        return lax.dot_general(
            act_v[k], grads_v[...], (((0,), (0,)), ((), ())), preferred_element_type=F32
        )

    def chunk_rows(k):
        return pl.ds(pl.multiple_of(k * CHUNK, CHUNK), CHUNK)

    def peer_copy(k):
        rows = chunk_rows(k)
        return pltpu.make_async_remote_copy(
            src_ref=peer_tx.at[rows],
            dst_ref=peer_rx.at[rows],
            send_sem=peer_send.at[0],
            recv_sem=peer_recv.at[0],
            device_id={"dp": dp, "rep": other},
            device_id_type=MESH,
        )

    load_grads.wait()

    @pl.loop(0, CHUNKS)
    def _(k):
        peer_tx[chunk_rows(k)] = product(k).astype(BF16)
        peer_copy(k).start()

    def for_own(lo, hi):
        @pl.loop(lo, hi)
        def _(k):
            own_g[chunk_rows(k)] = product(k + CHUNKS)

    for_own(0, 4)

    def compress(lo, hi, place):
        @pl.loop(lo * 2, hi * 2)
        def _(t):
            dx, dy = place(t // 2)
            xx, yy = lax.rem(x + dx, NX), lax.rem(y + dy, NY)
            for k in range(NZ // 2):
                zz = lax.rem(t, 2) * (NZ // 2) + k
                rows = pl.ds(pl.multiple_of(dp_at(zz, yy, xx) * OWN, OWN), OWN)
                at = [(xx * RING + yy) * NZ + zz, (yy * RING + xx) * NZ + zz]
                gradient = (own_g[rows, :] + peer_rx[rows, :].astype(F32)) * factor
                base = gradient + werr_v[rows, :].astype(F32)
                combined = [
                    beta_one * mom[i, at[i]].astype(F32) + base[:, part.columns]
                    for i, part in enumerate(parts)
                ]
                size = jnp.abs(combined[0]) + jnp.abs(combined[1])
                scale = jnp.sum(size, axis=1, keepdims=True) * (1.0 / WIDTH) + tiny_scale
                inverse = 1.0 / scale
                for i, part in enumerate(parts):
                    codes = jnp.clip(combined[i] * inverse, -1.0, 1.0).astype(BF16)
                    decoded = codes.astype(F32) * scale
                    left_v[rows, part.columns] = (combined[i] - decoded).astype(BF16)
                    dec[i, at[i]] = decoded.astype(BF16)

    def skip_two(k):
        return k + k // 2

    def finish_gradient():
        for_own(4, 8)
        load_werr.wait()
        pltpu.make_async_copy(peer_rx, peer_rx, peer_recv.at[0]).wait()

    def compress_own():
        compress(0, 1, lambda t: (0, 0))

    def compress_near():
        compress(1, 9, lambda t: (skip_two(t // 3), skip_two(lax.rem(t, 3))))

    def compress_far():
        compress(0, 4, lambda t: (2, t))
        compress(0, 3, lambda t: (skip_two(t), 2))

    gather_rest(gathers, finish_gradient, compress_own, compress_near, compress_far)

    reduces = [
        Reduce(
            part, dec.at[i], z, 3 * i + 1, 4 * G_COUNT + i * R_COUNT, near.at[i], far.at[i],
            partial.at[i], mids.at[i], sums.at[i], rounded.at[i], firsts.at[i],
        )
        for i, part in enumerate(parts)
    ]
    rows = (1, 2, 3, 0)
    for row in rows:
        for r in reduces:
            r.last_far(row)
    for row in rows:
        for r in reduces:
            r.last_own(row)
    store_left = pltpu.make_async_copy(left_v, left_out, out_sems.at[0])
    store_left.start()

    @pl.loop(0, RING)
    def _(t):
        for r in reduces:
            r.last_relay(lax.rem(t + 1, RING))

    @pl.loop(1, RING)
    def _(row):
        for r in reduces:
            r.mid(row)

    for r in reduces:
        r.mid_own()
    for r in reduces:
        r.first(dp_z)
    load_serr.wait()
    load_master.wait()
    load_variance.wait()
    summed = [r.total() for r in reduces]

    shifted = [
        summed[i] * (1.0 / (NX * NY * NZ)) + serr_v[:, part.columns]
        for i, part in enumerate(parts)
    ]
    size = jnp.abs(shifted[0]) + jnp.abs(shifted[1])
    scale = jnp.sum(size, axis=1, keepdims=True) * (1.0 / WIDTH) + tiny_scale
    gathers_w = []
    for i, part in enumerate(parts):
        codes = jnp.clip(shifted[i] / scale, -1.0, 1.0).astype(BF16)
        codes_v[:, part.columns] = codes
        momentum = codes.astype(F32) * scale
        server_v[:, part.columns] = shifted[i] - momentum
        new = master_v[:, part.columns] - learn_rate * momentum / (
            jnp.sqrt(variance_v[:, part.columns]) + tiny_root
        )
        new_master_v[:, part.columns] = new
        part.shard(wts.at[i], part.p, part.q, z)[...] = new.astype(BF16)
        g = Gather(part, wts.at[i], z, 3 * i + 2, (2 + i) * G_COUNT)
        g.first(dp_z)
        gathers_w.append(g)
    scale_out[...] = jnp.sum(
        jnp.where(eye, jnp.broadcast_to(scale, (OWN, OWN)), 0.0), axis=0, keepdims=True
    )
    stores = [
        store_left,
        pltpu.make_async_copy(codes_v, codes_out, out_sems.at[1]),
        pltpu.make_async_copy(server_v, server_out, out_sems.at[2]),
        pltpu.make_async_copy(new_master_v, master_out, out_sems.at[3]),
    ]
    for copy in stores[1:]:
        copy.start()

    def place(row):
        for i, g in enumerate(gathers_w):
            q = g.part.at_q(row)
            for p in range(RING):
                xx, yy = (p, q) if i == 0 else (q, p)
                pltpu.make_async_copy(
                    g.part.block(g.buf, p, q),
                    weights_out.at[:, yy, xx, :, pl.ds(i * PART, PART)],
                    out_sems.at[4],
                ).start()

    def place_near():
        for row in (0, 3, 1):
            place(row)

    gather_rest(gathers_w, lambda: None, lambda: None, place_near, lambda: place(2))
    pltpu.make_async_copy(weights_out, weights_out, out_sems.at[4]).wait()
    for copy in stores:
        copy.wait()
    for g in gathers + gathers_w + reduces:
        g.drain()
    pltpu.make_async_copy(peer_tx, peer_tx, peer_send.at[0]).wait()


def copy_kernel(count, *refs):
    sources, targets, rooms = refs[:count], refs[count : 2 * count], refs[2 * count : 3 * count]
    sems = refs[-1]
    pieces = []
    for i in range(count):
        rows = sources[i].shape[0]
        step = max(rows // 8, 1) if rows > OWN else rows
        pieces += [(i, k, step) for k in range(0, rows, step)]

    def copies(n):
        i, k, step = pieces[n]
        at = pl.ds(k, step)
        return (
            pltpu.make_async_copy(sources[i].at[at], rooms[i].at[at], sems.at[0, n]),
            pltpu.make_async_copy(rooms[i].at[at], targets[i].at[at], sems.at[1, n]),
        )

    for n in range(len(pieces)):
        copies(n)[0].start()
    for n in range(len(pieces)):
        copies(n)[0].wait()
        copies(n)[1].start()
    for n in range(len(pieces)):
        copies(n)[1].wait()


def copied(arrays):
    spec = pl.BlockSpec(memory_space=pltpu.HBM)
    return pl.pallas_call(
        functools.partial(copy_kernel, len(arrays)),
        out_shape=[jax.ShapeDtypeStruct(a.shape, a.dtype) for a in arrays],
        in_specs=[spec] * len(arrays),
        out_specs=[spec] * len(arrays),
        scratch_shapes=[pltpu.VMEM(a.shape, a.dtype) for a in arrays]
        + [pltpu.SemaphoreType.DMA((2, 20))],
        compiler_params=pltpu.CompilerParams(vmem_limit_bytes=56 * 1024 * 1024),
        name="hand_out",
    )(*arrays)


def body(act, grads, werr, mcodes, mscale, serr, master, variance):
    tokens = act.shape[0]
    hbm = pl.BlockSpec(memory_space=pltpu.HBM)
    vmem = pl.BlockSpec(memory_space=pltpu.VMEM)
    shards = NX * NY * NZ
    tile = (OWN, PART)

    def vm(*shape, dtype=BF16):
        return pltpu.VMEM(shape, dtype)

    scratch = [
        vm(2 * CHUNKS, tokens, CHUNK),
        vm(tokens, WIDTH),
        vm(HALF, WIDTH),
        vm(OWN, WIDTH),
        vm(OWN, WIDTH, dtype=F32),
        vm(OWN, WIDTH, dtype=F32),
        vm(OWN, WIDTH, dtype=F32),
        vm(HALF, WIDTH),
        vm(OWN, WIDTH),
        vm(OWN, WIDTH, dtype=F32),
        vm(OWN, WIDTH, dtype=F32),
        vm(HALF, WIDTH, dtype=F32),
        vm(HALF, WIDTH),
        vm(HALF, WIDTH),
        vm(2, shards, *tile),
        vm(2, shards, *tile),
        vm(2, shards, *tile),
        vm(2, RING, 2, NZ // 2, *tile),
        vm(2, RING, 2 * NZ, *tile),
        vm(2, RING, NZ, *tile),
        vm(2, (RING - 1) * NZ, *tile),
        vm(2, NZ, *tile, dtype=F32),
        vm(2, NZ, *tile),
        vm(2, NZ - 1, *tile),
    ]
    dma = pltpu.SemaphoreType.DMA
    scratch += [
        dma((6,)),
        dma((2 * CHUNKS,)),
        dma((5,)),
        dma((1,)),
        dma((1,)),
        dma((6,)),
        dma((4 * G_COUNT + 2 * R_COUNT,)),
    ]
    shape = jax.ShapeDtypeStruct
    outs = pl.pallas_call(
        step_kernel,
        out_shape=[
            shape((HALF, WIDTH), BF16),
            shape((OWN, WIDTH), BF16),
            shape((1, OWN), F32),
            shape((OWN, WIDTH), F32),
            shape((OWN, WIDTH), F32),
            shape((NZ, NY, NX, OWN, WIDTH), BF16),
        ],
        in_specs=[hbm] * 4 + [vmem] + [hbm] * 3,
        out_specs=[hbm, hbm, vmem, hbm, hbm, hbm],
        scratch_shapes=scratch,
        compiler_params=pltpu.CompilerParams(
            collective_id=0, has_side_effects=True, vmem_limit_bytes=56 * 1024 * 1024
        ),
        cost_estimate=pl.CostEstimate(
            flops=2 * tokens * 2 * HALF * WIDTH, bytes_accessed=14_000_000, transcendentals=0
        ),
        name="adam_step",
    )(act, grads, werr[0], mcodes, mscale.reshape(1, OWN), serr, master, variance)
    outs = [*outs[:-1], outs[-1].reshape(HALF, WIDTH)]
    left, codes, scale, server, new_master, weights = copied(outs)
    return (
        left[None],
        codes,
        scale.reshape(OWN),
        server,
        new_master,
        weights,
    )


def solution(mesh):
    return jax.shard_map(
        body,
        mesh=mesh,
        in_specs=(
            P(("dp", "rep"), None),
            P(("dp", "rep"), None),
            P("dp", "rep", None),
            P(("rep", "dp"), None),
            P(("rep", "dp")),
            P(("rep", "dp"), None),
            P(("rep", "dp"), None),
            P(("rep", "dp"), None),
        ),
        out_specs=(
            P("dp", "rep", None),
            P(("rep", "dp"), None),
            P(("rep", "dp")),
            P(("rep", "dp"), None),
            P(("rep", "dp"), None),
            P("rep", None),
        ),
        check_vma=False,
    )
```

time: 557 us -> 84 us (0.15)
  blocking collectives: 348 us -> 0 us
  waiting for transfers between devices: 148 us -> 0 us
  Pallas kernels: 0 us -> 83 us
  starting transfers between devices: 18.7 us -> 0 us
  between operations: 16.3 us -> 0.64 us
  other arithmetic: 11.1 us -> 0 us
  matrix products: 8.58 us -> 0 us
  local copies, waits for them, and re-layouts: 5.61 us -> 0 us
    unnamed x1 -> x0, blocking collectives: 348 us -> none
    all_gather x2 -> x0, waiting for transfers between devices: 109 us -> none  [the longest x1 109 us: body(): lax.all_gather(next_master.astype(jnp.bfloat16), 'dp', axis=0, tiled=True)]
    pallas_call x0 -> x2, Pallas kernels: none -> 83 us  [the longest x1 79 us: body(): pl.pallas_call(step_kernel, out_shape=[shape((HALF, WIDTH), BF16), shape(...]
    all_to_all x2 -> x0, waiting for transfers between devices: 38.5 us -> none  [the longest x1 31.1 us: body(): lax.all_to_all(sent_codes.reshape(owner_count, own_count, -1), 'dp', spli...]
    all_to_all x2 -> x0, starting transfers between devices: 18.6 us -> none  [the longest x1 11.9 us: body(): lax.all_to_all(sent_scale.reshape(owner_count, own_count).astype(jnp.bflo...]
    dot_general x1 -> x0, matrix products: 8.58 us -> none  [body(): jnp.dot(activations.T, out_grads, preferred_element_type=jnp.float32)]
  transfers between devices with their start and end apart: 5 -> 0, of which waited for: 3 -> 0; matrix products, arithmetic and copies ran while one was open for 3% -> 0% of each run, Pallas kernels for 0% -> 0%
where the time goes in v2:
time: 84 us; the launch traced here: 83.7 us
  Pallas kernels  83 us (99%)
    pallas_call x1, Pallas kernels, body(): pl.pallas_call(step_kernel, out_shape=[shape((HALF, WIDTH), BF16), shape(...  79 us
    pallas_call x1, Pallas kernels, copied(): pl.pallas_call(functools.partial(copy_kernel, len(arrays)), out_shape=[ja...  4 us

profile of v2, /device:TPU:2, one launch (start us, length us, event | category | flops | bytes accessed | tf_op | source)
XLA Modules:
  0.0 83.7 jit_solution(10855114926512101488)
XLA Ops:
  0.6 79.0 %adam_step.1 = (bf16[2048,512]{1,0:T(8,128)(2,1)}, bf16[16,512]{1,0:T(8,128)(2,1)}, f32[1,16]{1,0:T(1,128)}, f32[16,512]{1,0:T(8,128)}, f32[16,512]{1,0:T(8,128)}, /*index=5*/bf16[8,4,4,16,512]{4,3,2,1,0:T(8,128)(2,1)}) custom-call(bf16[736,4096]{1,0:T(8,128)(2,1)} %act.1, bf16[736,512]{1,0:T(8,128)(2,1)} %grads.1, bf16[2048,512]{1,0:T(8,128)(2,1)} %bitcast.6, ...), custom_call_target="tpu_custom_call" | custom-call | flops 3087007744 | bytes 14000000 | tf_op jit(solution)/shard_map/adam_step/pallas_call | solution.py:580
  79.7 4.0 %hand_out.1 = (bf16[2048,512]{1,0:T(8,128)(2,1)}, bf16[16,512]{1,0:T(8,128)(2,1)}, f32[1,16]{1,0:T(1,128)}, f32[16,512]{1,0:T(8,128)}, f32[16,512]{1,0:T(8,128)}, /*index=5*/bf16[2048,512]{1,0:T(8,128)(2,1)}) custom-call(bf16[2048,512]{1,0:T(8,128)(2,1)} %get-tuple-element.18.refs_0_, bf16[16,512]{1,0:T(8,128)(2,1)} %get-tuple-element.19.refs_1_, ...), custom_call_target="tpu_custom_call" | custom-call | tf_op jit(solution)/shard_map/hand_out/pallas_call | solution.py:521

commit v3 on v2

--- a/solution.py
+++ b/solution.py
@@ -66,9 +66,8 @@
         pltpu.make_async_copy(like, like, self.send_sems.at[send]).wait()
 
 
-G_FIRST, G_MID, G_LEFT, G_RIGHT, G_REST, G_COUNT = 0, 0, 4, 8, 12, 16
-R_FIRST, R_MID, R_LEFT, R_RIGHT, R_REST, R_COUNT = 0, 1, 2, 6, 10, 14
-G_SENDS, R_SENDS = 0, 1
+G_FIRST, G_MID, G_ROW, G_COUNT = 0, 0, 4, 8
+R_FIRST, R_MID, R_ROW, R_COUNT = 0, 1, 2, 6
 
 
 class Gather:
@@ -80,7 +79,7 @@
 
     def first(self, dp_z):
         mine = self.part.shard(self.buf, self.part.p, self.part.q, self.z)
-        for k in range(1, NZ):
+        for k in (4, 3, 5, 2, 6, 1, 7):
             self.go(mine, G_FIRST, dp_z(lax.rem(self.z + k, NZ)))
 
     def first_here(self):
@@ -88,7 +87,7 @@
 
     def mid(self):
         part = self.part
-        for k in (1, 3, 2):
+        for k in (2, 1, 3):
             self.go(part.block(self.buf, part.p, part.q), G_MID + k, part.dp_pq(part.p, part.at_q(k)))
 
     def mid_here(self, k):
@@ -97,113 +96,66 @@
 
     def last(self, row):
         part = self.part
-        q = part.at_q(row)
-        lower, upper = part.half(self.buf, part.p, q, 0), part.half(self.buf, part.p, q, 1)
-        after = part.dp_pq(part.at_p(1), part.q)
-        before = part.dp_pq(part.at_p(-1), part.q)
-        self.go(lower, G_LEFT + row, after)
-        self.go(upper, G_RIGHT + row, before)
-        self.go(upper, G_REST + row, after)
-        self.go(lower, G_REST + row, before)
-
-    def relay(self, row):
-        part = self.part
-        q = part.at_q(row)
-        lower = part.half(self.buf, part.at_p(-1), q, 0)
-        part.wait(lower, self.recv + G_LEFT + row)
-        self.go(lower, G_REST + row, part.dp_pq(part.at_p(1), part.q))
-        upper = part.half(self.buf, part.at_p(1), q, 1)
-        part.wait(upper, self.recv + G_RIGHT + row)
-        self.go(upper, G_REST + row, part.dp_pq(part.at_p(-1), part.q))
+        block = part.block(self.buf, part.p, part.at_q(row))
+        for k in (2, 1, 3):
+            self.go(block, G_ROW + row, part.dp_pq(part.at_p(k), part.q))
 
     def row_here(self, row):
-        self.part.wait(self.buf.at[pl.ds(0, 2 * NZ)], self.recv + G_REST + row)
+        self.part.wait(self.buf.at[pl.ds(0, 3 * NZ)], self.recv + G_ROW + row)
 
     def drain(self):
         self.part.drain(self.buf.at[pl.ds(0, NX * NY * NZ - 1)], self.send_sem)
 
 
-def gather_rest(gathers, before_blocks, own_block, near_rows, all_rows):
+def gather_rest(gathers, first_sent, own_block, near_rows, all_rows):
     for g in gathers:
         g.first_here()
     for g in gathers:
         g.mid()
         g.last(0)
-    before_blocks()
+    first_sent()
     for k in (1, 3):
         for g in gathers:
             g.mid_here(k)
             g.last(RING - k)
     for g in gathers:
-        g.relay(0)
-    for g in gathers:
         g.mid_here(2)
         g.last(2)
     own_block()
-    for row in (3, 1):
-        for g in gathers:
-            g.relay(row)
     for row in (0, 3, 1):
         for g in gathers:
             g.row_here(row)
     near_rows()
     for g in gathers:
-        g.relay(2)
-    for g in gathers:
         g.row_here(2)
     all_rows()
 
 
 class Reduce:
-    def __init__(self, part, dec, z, send, recv, near, far, partial, mids, sums, rounded, firsts):
+    def __init__(self, part, dec, z, send, recv, far, partial, mids, sums, rounded, firsts):
         self.part, self.dec, self.z, self.send_sem, self.recv = part, dec, z, send, recv
-        self.near, self.far, self.partial = near, far, partial
+        self.far, self.partial = far, partial
         self.mids, self.sums, self.rounded, self.firsts = mids, sums, rounded, firsts
 
     def go(self, src, dst, recv, dp):
         self.part.send(src, dst, self.send_sem, self.recv + recv, dp)
 
-    def steps(self, row):
+    def last(self, row, k):
         part = self.part
-        return (
-            part.at_q(row),
-            part.dp_pq(part.at_p(1), part.q),
-            part.dp_pq(part.at_p(-1), part.q),
-        )
-
-    def half_of(self, row, way, which):
-        return self.far.at[row, pl.ds(way * NZ + which * (NZ // 2), NZ // 2)]
-
-    def last_far(self, row):
-        part = self.part
-        q, after, before = self.steps(row)
-        opposite = part.at_p(2)
-        self.go(part.half(self.dec, opposite, q, 0), self.near.at[row, 0], R_LEFT + row, after)
-        self.go(part.half(self.dec, opposite, q, 1), self.near.at[row, 1], R_RIGHT + row, before)
-
-    def last_own(self, row):
-        part = self.part
-        q, after, before = self.steps(row)
-        self.go(part.half(self.dec, part.at_p(1), q, 1), self.half_of(row, 0, 1), R_REST + row, after)
-        self.go(part.half(self.dec, part.at_p(-1), q, 0), self.half_of(row, 1, 0), R_REST + row, before)
-
-    def last_relay(self, row):
-        part = self.part
-        q, after, before = self.steps(row)
-        for way, sem, to, dp in ((0, R_LEFT, 1, after), (1, R_RIGHT, -1, before)):
-            got = self.near.at[row, way]
-            part.wait(got, self.recv + sem + row)
-            mine = part.half(self.dec, part.at_p(to), q, way)
-            mine[...] = (mine[...].astype(F32) + got[...].astype(F32)).astype(BF16)
-            self.go(mine, self.half_of(row, way, way), R_REST + row, dp)
+        self.go(
+            part.block(self.dec, part.at_p(k), part.at_q(row)),
+            self.far.at[row, pl.ds((k - 1) * NZ, NZ)],
+            R_ROW + row,
+            part.dp_pq(part.at_p(k), part.q),
+        )
 
     def row_total(self, row):
         part = self.part
-        part.wait(self.far.at[row], self.recv + R_REST + row)
+        part.wait(self.far.at[row], self.recv + R_ROW + row)
         total = part.block(self.dec, part.p, part.at_q(row))[...].astype(F32)
-        return total + (
-            self.far[row, pl.ds(0, NZ)].astype(F32) + self.far[row, pl.ds(NZ, NZ)].astype(F32)
-        )
+        for k in range(RING - 1):
+            total += self.far[row, pl.ds(k * NZ, NZ)].astype(F32)
+        return total
 
     def mid(self, row):
         part = self.part
@@ -246,7 +198,7 @@
     act_v, grads_v, werr_v, mcodes_v, serr_v, master_v, variance_v,
     left_v, codes_v, server_v, new_master_v,
     own_g, peer_tx, peer_rx,
-    mom, dec, wts, near, far, partial, mids, sums, rounded, firsts,
+    mom, dec, wts, far, partial, mids, sums, rounded, firsts,
     in_sems, act_sems, out_sems, peer_send, peer_recv, send_sems, recv_sems,
 ):
     dp = lax.axis_index("dp")
@@ -306,7 +258,7 @@
         jnp.where(eye, jnp.broadcast_to(mscale[...], (OWN, OWN)), 0.0), axis=1, keepdims=True
     )
     load_codes.wait()
-    previous = (mcodes_v[...].astype(F32) * scale_col).astype(BF16)
+    previous = (mcodes_v[...].astype(F32) * (beta_one * scale_col)).astype(BF16)
 
     parts = [
         Part(0, x, y, lambda p, q: dp_at(z, q, p), core, send_sems, recv_sems),
@@ -344,14 +296,16 @@
 
     @pl.loop(0, CHUNKS)
     def _(k):
-        peer_tx[chunk_rows(k)] = product(k).astype(BF16)
+        peer_tx[chunk_rows(k)] = (product(k) * factor).astype(BF16)
         peer_copy(k).start()
 
     def for_own(lo, hi):
         @pl.loop(lo, hi)
         def _(k):
-            own_g[chunk_rows(k)] = product(k + CHUNKS)
-
+            rows = chunk_rows(k)
+            own_g[rows] = product(k + CHUNKS) * factor + werr_v[rows].astype(F32)
+
+    load_werr.wait()
     for_own(0, 4)
 
     def compress(lo, hi, place):
@@ -363,10 +317,8 @@
                 zz = lax.rem(t, 2) * (NZ // 2) + k
                 rows = pl.ds(pl.multiple_of(dp_at(zz, yy, xx) * OWN, OWN), OWN)
                 at = [(xx * RING + yy) * NZ + zz, (yy * RING + xx) * NZ + zz]
-                gradient = (own_g[rows, :] + peer_rx[rows, :].astype(F32)) * factor
-                base = gradient + werr_v[rows, :].astype(F32)
                 combined = [
-                    beta_one * mom[i, at[i]].astype(F32) + base[:, part.columns]
+                    mom[i, at[i]].astype(F32) + own_g[rows, part.columns]
                     for i, part in enumerate(parts)
                 ]
                 size = jnp.abs(combined[0]) + jnp.abs(combined[1])
@@ -383,45 +335,48 @@
 
     def finish_gradient():
         for_own(4, 8)
-        load_werr.wait()
         pltpu.make_async_copy(peer_rx, peer_rx, peer_recv.at[0]).wait()
 
     def compress_own():
+        @pl.loop(0, HALF // 64)
+        def _(t):
+            rows = pl.ds(pl.multiple_of(t * 64, 64), 64)
+            own_g[rows] += peer_rx[rows].astype(F32)
+
         compress(0, 1, lambda t: (0, 0))
+
+    reduces = [
+        Reduce(
+            part, dec.at[i], z, 3 * i + 1, 4 * G_COUNT + i * R_COUNT, far.at[i],
+            partial.at[i], mids.at[i], sums.at[i], rounded.at[i], firsts.at[i],
+        )
+        for i, part in enumerate(parts)
+    ]
 
     def compress_near():
         compress(1, 9, lambda t: (skip_two(t // 3), skip_two(lax.rem(t, 3))))
+        for row in (3, 1, 0):
+            for r in reduces:
+                r.last(row, 1)
+                r.last(row, 3)
 
     def compress_far():
         compress(0, 4, lambda t: (2, t))
         compress(0, 3, lambda t: (skip_two(t), 2))
 
     gather_rest(gathers, finish_gradient, compress_own, compress_near, compress_far)
-
-    reduces = [
-        Reduce(
-            part, dec.at[i], z, 3 * i + 1, 4 * G_COUNT + i * R_COUNT, near.at[i], far.at[i],
-            partial.at[i], mids.at[i], sums.at[i], rounded.at[i], firsts.at[i],
-        )
-        for i, part in enumerate(parts)
-    ]
-    rows = (1, 2, 3, 0)
-    for row in rows:
+    for row in (2, 3, 1, 0):
         for r in reduces:
-            r.last_far(row)
-    for row in rows:
-        for r in reduces:
-            r.last_own(row)
+            r.last(row, 2)
+            if row == 2:
+                r.last(row, 1)
+                r.last(row, 3)
     store_left = pltpu.make_async_copy(left_v, left_out, out_sems.at[0])
     store_left.start()
 
-    @pl.loop(0, RING)
+    @pl.loop(0, RING - 1)
     def _(t):
-        for r in reduces:
-            r.last_relay(lax.rem(t + 1, RING))
-
-    @pl.loop(1, RING)
-    def _(row):
+        row = lax.rem(2 + t, RING) + t // 2
         for r in reduces:
             r.mid(row)
 
@@ -491,41 +446,22 @@
 
 
 def copy_kernel(count, *refs):
-    sources, targets, rooms = refs[:count], refs[count : 2 * count], refs[2 * count : 3 * count]
-    sems = refs[-1]
-    pieces = []
-    for i in range(count):
-        rows = sources[i].shape[0]
-        step = max(rows // 8, 1) if rows > OWN else rows
-        pieces += [(i, k, step) for k in range(0, rows, step)]
-
-    def copies(n):
-        i, k, step = pieces[n]
-        at = pl.ds(k, step)
-        return (
-            pltpu.make_async_copy(sources[i].at[at], rooms[i].at[at], sems.at[0, n]),
-            pltpu.make_async_copy(rooms[i].at[at], targets[i].at[at], sems.at[1, n]),
-        )
-
-    for n in range(len(pieces)):
-        copies(n)[0].start()
-    for n in range(len(pieces)):
-        copies(n)[0].wait()
-        copies(n)[1].start()
-    for n in range(len(pieces)):
-        copies(n)[1].wait()
+    sources, targets, sems = refs[:count], refs[count : 2 * count], refs[-1]
+    copies = [pltpu.make_async_copy(sources[i], targets[i], sems.at[i]) for i in range(count)]
+    for copy in copies:
+        copy.start()
+    for copy in copies:
+        copy.wait()
 
 
 def copied(arrays):
-    spec = pl.BlockSpec(memory_space=pltpu.HBM)
     return pl.pallas_call(
         functools.partial(copy_kernel, len(arrays)),
         out_shape=[jax.ShapeDtypeStruct(a.shape, a.dtype) for a in arrays],
-        in_specs=[spec] * len(arrays),
-        out_specs=[spec] * len(arrays),
-        scratch_shapes=[pltpu.VMEM(a.shape, a.dtype) for a in arrays]
-        + [pltpu.SemaphoreType.DMA((2, 20))],
-        compiler_params=pltpu.CompilerParams(vmem_limit_bytes=56 * 1024 * 1024),
+        in_specs=[pl.BlockSpec(memory_space=pltpu.VMEM)] * len(arrays),
+        out_specs=[pl.BlockSpec(memory_space=pltpu.HBM)] * len(arrays),
+        scratch_shapes=[pltpu.SemaphoreType.DMA((len(arrays),))],
+        compiler_params=pltpu.CompilerParams(vmem_limit_bytes=16 * 1024 * 1024),
         name="hand_out",
     )(*arrays)
 
@@ -558,8 +494,7 @@
         vm(2, shards, *tile),
         vm(2, shards, *tile),
         vm(2, shards, *tile),
-        vm(2, RING, 2, NZ // 2, *tile),
-        vm(2, RING, 2 * NZ, *tile),
+        vm(2, RING, (RING - 1) * NZ, *tile),
         vm(2, RING, NZ, *tile),
         vm(2, (RING - 1) * NZ, *tile),
         vm(2, NZ, *tile, dtype=F32),
@@ -576,7 +511,7 @@
         dma((6,)),
         dma((4 * G_COUNT + 2 * R_COUNT,)),
     ]
-    shape = jax.ShapeDtypeStruct
+    shape = pltpu.VMEM
     outs = pl.pallas_call(
         step_kernel,
         out_shape=[
@@ -588,10 +523,10 @@
             shape((NZ, NY, NX, OWN, WIDTH), BF16),
         ],
         in_specs=[hbm] * 4 + [vmem] + [hbm] * 3,
-        out_specs=[hbm, hbm, vmem, hbm, hbm, hbm],
+        out_specs=[vmem] * 6,
         scratch_shapes=scratch,
         compiler_params=pltpu.CompilerParams(
-            collective_id=0, has_side_effects=True, vmem_limit_bytes=56 * 1024 * 1024
+            collective_id=0, has_side_effects=True, vmem_limit_bytes=54 * 1024 * 1024
         ),
         cost_estimate=pl.CostEstimate(
             flops=2 * tokens * 2 * HALF * WIDTH, bytes_accessed=14_000_000, transcendentals=0

time: 84 us -> 77.9 us (0.927)
  Pallas kernels: 83 us -> 77.1 us
    pallas_call x1, Pallas kernels: 79 us -> 75 us  [body(): pl.pallas_call(step_kernel, out_shape=[shape((HALF, WIDTH), BF16), shape(...]
    pallas_call x1, Pallas kernels: 4 us -> 2.1 us  [copied(): pl.pallas_call(functools.partial(copy_kernel, len(arrays)), out_shape=[ja...]
where the time goes in v3:
time: 77.9 us; the launch traced here: 77.8 us
  Pallas kernels  77.1 us (99%)
    pallas_call x1, Pallas kernels, body(): pl.pallas_call(step_kernel, out_shape=[shape((HALF, WIDTH), BF16), shape(...  75 us
    pallas_call x1, Pallas kernels, copied(): pl.pallas_call(functools.partial(copy_kernel, len(arrays)), out_shape=[ja...  2.1 us

profile of v3, /device:TPU:2, one launch (start us, length us, event | category | flops | bytes accessed | tf_op | source)
XLA Modules:
  0.0 77.8 jit_solution(1218343011434999766)
XLA Ops:
  0.6 75.0 %adam_step.1 = (bf16[2048,512]{1,0:T(8,128)(2,1)S(1)}, bf16[16,512]{1,0:T(8,128)(2,1)S(1)}, f32[1,16]{1,0:T(1,128)S(1)}, f32[16,512]{1,0:T(8,128)S(1)}, f32[16,5...) custom-call(bf16[736,4096]{1,0:T(8,128)(2,1)} %act.1, bf16[736,512]{1,0:T(8,128)(2,1)} %grads.1, ...), custom_call_target="tpu_custom_call" | custom-call | flops 3087007744 | bytes 14000000 | tf_op jit(solution)/shard_map/adam_step/pallas_call | solution.py:515
  75.7 2.1 %hand_out.1 = (bf16[2048,512]{1,0:T(8,128)(2,1)}, bf16[16,512]{1,0:T(8,128)(2,1)}, f32[1,16]{1,0:T(1,128)}, f32[16,512]{1,0:T(8,128)}, f32[16,512]{1,0:T(8,128)}, /*index=5*/bf16[2048,512]{1,0:T(8,128)(2,1)}) custom-call(bf16[2048,512]{1,0:T(8,128)(2,1)S(1)} %get-tuple-element.18.refs_0_, bf16[16,512]{1,0:T(8,128)(2,1)S(1)} %get-tuple-element.19.refs_1_, ...), custom_call_target="tpu_custom_call" | custom-call | tf_op jit(solution)/shard_map/hand_out/pallas_call | solution.py:458

commit v4 on v3

--- a/solution.py
+++ b/solution.py
@@ -15,7 +15,10 @@
 NX, NY, NZ = 4, 4, 8
 RING = 4
 OWN = 16
+GROUPS = 2
+ROWS = OWN // GROUPS
 PART = 256
+LANES = PART // GROUPS
 CHUNK = 256
 HALF = 2048
 WIDTH = 512
@@ -29,7 +32,8 @@
 
 
 class Part:
-    def __init__(self, column, p, q, dp_pq, core, send_sems, recv_sems):
+    def __init__(self, group, column, p, q, dp_pq, core, send_sems, recv_sems):
+        self.rows = slice(group * ROWS, (group + 1) * ROWS)
         self.columns = slice(column, column + PART)
         self.p, self.q, self.dp_pq, self.core = p, q, dp_pq, core
         self.send_sems, self.recv_sems = send_sems, recv_sems
@@ -70,6 +74,18 @@
 R_FIRST, R_MID, R_ROW, R_COUNT = 0, 1, 2, 6
 
 
+def packed(rows):
+    return jnp.concatenate([rows[:, :LANES], rows[:, LANES:]], axis=0).astype(BF16)
+
+
+def unpacked_sum(wide):
+    return jnp.concatenate([wide[:ROWS], wide[ROWS:]], axis=1)
+
+
+def unpacked(tile):
+    return unpacked_sum(tile.astype(F32))
+
+
 class Gather:
     def __init__(self, part, buf, z, send, recv):
         self.part, self.buf, self.z, self.send_sem, self.recv = part, buf, z, send, recv
@@ -107,28 +123,25 @@
         self.part.drain(self.buf.at[pl.ds(0, NX * NY * NZ - 1)], self.send_sem)
 
 
-def gather_rest(gathers, first_sent, own_block, near_rows, all_rows):
+def begin(gathers):
     for g in gathers:
         g.first_here()
     for g in gathers:
         g.mid()
         g.last(0)
-    first_sent()
-    for k in (1, 3):
+
+
+def spread(gathers):
+    for k in (1, 3, 2):
         for g in gathers:
             g.mid_here(k)
             g.last(RING - k)
-    for g in gathers:
-        g.mid_here(2)
-        g.last(2)
-    own_block()
-    for row in (0, 3, 1):
+
+
+def here(gathers, rows):
+    for row in rows:
         for g in gathers:
             g.row_here(row)
-    near_rows()
-    for g in gathers:
-        g.row_here(2)
-    all_rows()
 
 
 class Reduce:
@@ -196,10 +209,9 @@
     act, grads, werr, mcodes, mscale, serr, master, variance,
     left_out, codes_out, scale_out, server_out, master_out, weights_out,
     act_v, grads_v, werr_v, mcodes_v, serr_v, master_v, variance_v,
-    left_v, codes_v, server_v, new_master_v,
-    own_g, peer_tx, peer_rx,
+    own_g, left_v, peer_tx, peer_rx,
     mom, dec, wts, far, partial, mids, sums, rounded, firsts,
-    in_sems, act_sems, out_sems, peer_send, peer_recv, send_sems, recv_sems,
+    in_sems, act_sems, peer_send, peer_recv, send_sems, recv_sems,
 ):
     dp = lax.axis_index("dp")
     core = lax.axis_index("rep")
@@ -258,16 +270,36 @@
         jnp.where(eye, jnp.broadcast_to(mscale[...], (OWN, OWN)), 0.0), axis=1, keepdims=True
     )
     load_codes.wait()
-    previous = (mcodes_v[...].astype(F32) * (beta_one * scale_col)).astype(BF16)
-
-    parts = [
-        Part(0, x, y, lambda p, q: dp_at(z, q, p), core, send_sems, recv_sems),
-        Part(PART, y, x, lambda p, q: dp_at(z, p, q), core, send_sems, recv_sems),
-    ]
-    gathers = []
-    for i, part in enumerate(parts):
-        part.shard(mom.at[i], part.p, part.q, z)[...] = previous[:, part.columns]
-        gathers.append(Gather(part, mom.at[i], z, 3 * i, i * G_COUNT))
+    previous = mcodes_v[...].astype(F32) * (beta_one * scale_col)
+
+    def x_major(p, q):
+        return dp_at(z, q, p)
+
+    def y_major(p, q):
+        return dp_at(z, p, q)
+
+    parts = []
+    for group in range(GROUPS):
+        parts += [
+            Part(group, 0, x, y, x_major, core, send_sems, recv_sems),
+            Part(group, PART, y, x, y_major, core, send_sems, recv_sems),
+        ]
+    count = len(parts)
+
+    def by_group(items):
+        return [items[2 * group : 2 * group + 2] for group in range(GROUPS)]
+
+    gathers, gathers_w, reduces = [], [], []
+    for n, part in enumerate(parts):
+        part.shard(mom.at[n], part.p, part.q, z)[...] = packed(previous[part.rows, part.columns])
+        gathers.append(Gather(part, mom.at[n], z, 3 * n, n * G_COUNT))
+        gathers_w.append(Gather(part, wts.at[n], z, 3 * n + 2, (count + n) * G_COUNT))
+        reduces.append(
+            Reduce(
+                part, dec.at[n], z, 3 * n + 1, 2 * count * G_COUNT + n * R_COUNT, far.at[n],
+                partial.at[n], mids.at[n], sums.at[n], rounded.at[n], firsts.at[n],
+            )
+        )
     pl.semaphore_wait(barrier, len(peers))
     for g in gathers:
         g.first(dp_z)
@@ -308,138 +340,146 @@
     load_werr.wait()
     for_own(0, 4)
 
-    def compress(lo, hi, place):
-        @pl.loop(lo * 2, hi * 2)
+    for gs in by_group(gathers):
+        begin(gs)
+    for_own(4, 8)
+    for gs in by_group(gathers):
+        spread(gs)
+    pltpu.make_async_copy(peer_rx, peer_rx, peer_recv.at[0]).wait()
+
+    @pl.loop(0, HALF // 64)
+    def _(t):
+        rows = pl.ds(pl.multiple_of(t * 64, 64), 64)
+        own_g[rows] += peer_rx[rows].astype(F32)
+
+    def blocks(lo, hi, offsets, work):
+        @pl.loop(lo, hi)
         def _(t):
-            dx, dy = place(t // 2)
+            dx, dy = offsets(t)
             xx, yy = lax.rem(x + dx, NX), lax.rem(y + dy, NY)
-            for k in range(NZ // 2):
-                zz = lax.rem(t, 2) * (NZ // 2) + k
-                rows = pl.ds(pl.multiple_of(dp_at(zz, yy, xx) * OWN, OWN), OWN)
-                at = [(xx * RING + yy) * NZ + zz, (yy * RING + xx) * NZ + zz]
-                combined = [
-                    mom[i, at[i]].astype(F32) + own_g[rows, part.columns]
-                    for i, part in enumerate(parts)
-                ]
-                size = jnp.abs(combined[0]) + jnp.abs(combined[1])
-                scale = jnp.sum(size, axis=1, keepdims=True) * (1.0 / WIDTH) + tiny_scale
-                inverse = 1.0 / scale
-                for i, part in enumerate(parts):
-                    codes = jnp.clip(combined[i] * inverse, -1.0, 1.0).astype(BF16)
-                    decoded = codes.astype(F32) * scale
-                    left_v[rows, part.columns] = (combined[i] - decoded).astype(BF16)
-                    dec[i, at[i]] = decoded.astype(BF16)
+            work(yy, xx, [(xx * RING + yy) * NZ, (yy * RING + xx) * NZ])
 
     def skip_two(k):
         return k + k // 2
 
-    def finish_gradient():
-        for_own(4, 8)
-        pltpu.make_async_copy(peer_rx, peer_rx, peer_recv.at[0]).wait()
-
-    def compress_own():
-        @pl.loop(0, HALF // 64)
-        def _(t):
-            rows = pl.ds(pl.multiple_of(t * 64, 64), 64)
-            own_g[rows] += peer_rx[rows].astype(F32)
-
-        compress(0, 1, lambda t: (0, 0))
-
-    reduces = [
-        Reduce(
-            part, dec.at[i], z, 3 * i + 1, 4 * G_COUNT + i * R_COUNT, far.at[i],
-            partial.at[i], mids.at[i], sums.at[i], rounded.at[i], firsts.at[i],
-        )
-        for i, part in enumerate(parts)
-    ]
-
-    def compress_near():
-        compress(1, 9, lambda t: (skip_two(t // 3), skip_two(lax.rem(t, 3))))
+    def near_blocks(work):
+        blocks(0, 9, lambda t: (skip_two(t // 3), skip_two(lax.rem(t, 3))), work)
+
+    def far_blocks(work):
+        blocks(0, 4, lambda t: (2, t), work)
+        blocks(0, 3, lambda t: (skip_two(t), 2), work)
+
+    def compress(group, yy, xx, at):
+        rows = [
+            pl.ds(pl.multiple_of(dp_at(zz, yy, xx) * OWN + group * ROWS, ROWS), ROWS)
+            for zz in range(NZ)
+        ]
+        pair = (0, 1)
+        combined = [
+            [
+                unpacked(mom[2 * group + i, at[i] + zz]) + own_g[rows[zz], parts[i].columns]
+                for i in pair
+            ]
+            for zz in range(NZ)
+        ]
+        scales = []
+        for zz in range(NZ):
+            size = jnp.abs(combined[zz][0]) + jnp.abs(combined[zz][1])
+            total = jnp.sum(size, axis=1, keepdims=True)
+            scales.append(total * (1.0 / WIDTH) + tiny_scale)
+        for zz in range(NZ):
+            inverse = 1.0 / scales[zz]
+            for i in pair:
+                codes = jnp.clip(combined[zz][i] * inverse, -1.0, 1.0).astype(BF16)
+                decoded = codes.astype(F32) * scales[zz]
+                left_v[rows[zz], parts[i].columns] = combined[zz][i] - decoded
+                dec[2 * group + i, at[i] + zz] = packed(decoded)
+
+    near_rows = (0, 3, 1)
+    for group, (gs, rs) in enumerate(zip(by_group(gathers), by_group(reduces))):
+        work = functools.partial(compress, group)
+        here(gs, near_rows)
+        near_blocks(work)
         for row in (3, 1, 0):
-            for r in reduces:
+            for r in rs:
                 r.last(row, 1)
                 r.last(row, 3)
-
-    def compress_far():
-        compress(0, 4, lambda t: (2, t))
-        compress(0, 3, lambda t: (skip_two(t), 2))
-
-    gather_rest(gathers, finish_gradient, compress_own, compress_near, compress_far)
-    for row in (2, 3, 1, 0):
-        for r in reduces:
-            r.last(row, 2)
-            if row == 2:
-                r.last(row, 1)
-                r.last(row, 3)
-    store_left = pltpu.make_async_copy(left_v, left_out, out_sems.at[0])
-    store_left.start()
-
-    @pl.loop(0, RING - 1)
+        here(gs, (2,))
+        far_blocks(work)
+        for row in (2, 3, 1, 0):
+            for r in rs:
+                r.last(row, 2)
+                if row == 2:
+                    r.last(row, 1)
+                    r.last(row, 3)
+
+    @pl.loop(0, HALF // 64)
     def _(t):
-        row = lax.rem(2 + t, RING) + t // 2
-        for r in reduces:
-            r.mid(row)
-
-    for r in reduces:
-        r.mid_own()
-    for r in reduces:
-        r.first(dp_z)
+        rows = pl.ds(pl.multiple_of(t * 64, 64), 64)
+        left_out[rows] = left_v[rows].astype(BF16)
+
+    for rs in by_group(reduces):
+
+        @pl.loop(0, RING - 1)
+        def _(t):
+            row = lax.rem(2 + t, RING) + t // 2
+            for r in rs:
+                r.mid(row)
+
+        for r in rs:
+            r.mid_own()
+    for rs in by_group(reduces):
+        for r in rs:
+            r.first(dp_z)
     load_serr.wait()
     load_master.wait()
     load_variance.wait()
-    summed = [r.total() for r in reduces]
-
-    shifted = [
-        summed[i] * (1.0 / (NX * NY * NZ)) + serr_v[:, part.columns]
-        for i, part in enumerate(parts)
-    ]
-    size = jnp.abs(shifted[0]) + jnp.abs(shifted[1])
-    scale = jnp.sum(size, axis=1, keepdims=True) * (1.0 / WIDTH) + tiny_scale
-    gathers_w = []
-    for i, part in enumerate(parts):
-        codes = jnp.clip(shifted[i] / scale, -1.0, 1.0).astype(BF16)
-        codes_v[:, part.columns] = codes
-        momentum = codes.astype(F32) * scale
-        server_v[:, part.columns] = shifted[i] - momentum
-        new = master_v[:, part.columns] - learn_rate * momentum / (
-            jnp.sqrt(variance_v[:, part.columns]) + tiny_root
-        )
-        new_master_v[:, part.columns] = new
-        part.shard(wts.at[i], part.p, part.q, z)[...] = new.astype(BF16)
-        g = Gather(part, wts.at[i], z, 3 * i + 2, (2 + i) * G_COUNT)
-        g.first(dp_z)
-        gathers_w.append(g)
+
+    all_codes, all_scales = [], []
+    for group, (gs, rs) in enumerate(zip(by_group(gathers_w), by_group(reduces))):
+        rows = parts[2 * group].rows
+        shifted = [
+            unpacked_sum(r.total()) * (1.0 / (NX * NY * NZ)) + serr_v[rows, r.part.columns]
+            for r in rs
+        ]
+        size = jnp.abs(shifted[0]) + jnp.abs(shifted[1])
+        scale = jnp.sum(size, axis=1, keepdims=True) * (1.0 / WIDTH) + tiny_scale
+        for i, g in enumerate(gs):
+            columns = g.part.columns
+            codes = jnp.clip(shifted[i] / scale, -1.0, 1.0).astype(BF16).astype(F32)
+            all_codes.append(codes)
+            momentum = codes * scale
+            server_out[rows, columns] = shifted[i] - momentum
+            new = master_v[rows, columns] - learn_rate * momentum / (
+                jnp.sqrt(variance_v[rows, columns]) + tiny_root
+            )
+            master_out[rows, columns] = new
+            g.part.shard(g.buf, g.part.p, g.part.q, z)[...] = packed(new)
+            g.first(dp_z)
+        all_scales.append(scale)
+    for i in range(2):
+        codes_out[:, parts[i].columns] = jnp.concatenate(all_codes[i::2], axis=0).astype(BF16)
+    scale = jnp.concatenate(all_scales, axis=0)
     scale_out[...] = jnp.sum(
         jnp.where(eye, jnp.broadcast_to(scale, (OWN, OWN)), 0.0), axis=0, keepdims=True
     )
-    stores = [
-        store_left,
-        pltpu.make_async_copy(codes_v, codes_out, out_sems.at[1]),
-        pltpu.make_async_copy(server_v, server_out, out_sems.at[2]),
-        pltpu.make_async_copy(new_master_v, master_out, out_sems.at[3]),
-    ]
-    for copy in stores[1:]:
-        copy.start()
-
-    def place(row):
-        for i, g in enumerate(gathers_w):
-            q = g.part.at_q(row)
-            for p in range(RING):
-                xx, yy = (p, q) if i == 0 else (q, p)
-                pltpu.make_async_copy(
-                    g.part.block(g.buf, p, q),
-                    weights_out.at[:, yy, xx, :, pl.ds(i * PART, PART)],
-                    out_sems.at[4],
-                ).start()
-
-    def place_near():
-        for row in (0, 3, 1):
-            place(row)
-
-    gather_rest(gathers_w, lambda: None, lambda: None, place_near, lambda: place(2))
-    pltpu.make_async_copy(weights_out, weights_out, out_sems.at[4]).wait()
-    for copy in stores:
-        copy.wait()
+
+    def assemble(yy, xx, at):
+        for zz in range(NZ):
+            for i in range(2):
+                rows = [unpacked(wts[2 * group + i, at[i] + zz]) for group in range(GROUPS)]
+                weights_out[zz, yy, xx, :, parts[i].columns] = jnp.concatenate(
+                    rows, axis=0
+                ).astype(BF16)
+
+    for gs in by_group(gathers_w):
+        begin(gs)
+    for gs in by_group(gathers_w):
+        spread(gs)
+    here(gathers_w, near_rows)
+    near_blocks(assemble)
+    here(gathers_w, (2,))
+    far_blocks(assemble)
     for g in gathers + gathers_w + reduces:
         g.drain()
     pltpu.make_async_copy(peer_tx, peer_tx, peer_send.at[0]).wait()
@@ -471,7 +511,8 @@
     hbm = pl.BlockSpec(memory_space=pltpu.HBM)
     vmem = pl.BlockSpec(memory_space=pltpu.VMEM)
     shards = NX * NY * NZ
-    tile = (OWN, PART)
+    tile = (OWN, LANES)
+    count = 2 * GROUPS
 
     def vm(*shape, dtype=BF16):
         return pltpu.VMEM(shape, dtype)
@@ -484,32 +525,28 @@
         vm(OWN, WIDTH, dtype=F32),
         vm(OWN, WIDTH, dtype=F32),
         vm(OWN, WIDTH, dtype=F32),
-        vm(HALF, WIDTH),
-        vm(OWN, WIDTH),
-        vm(OWN, WIDTH, dtype=F32),
-        vm(OWN, WIDTH, dtype=F32),
+        vm(HALF, WIDTH, dtype=F32),
         vm(HALF, WIDTH, dtype=F32),
         vm(HALF, WIDTH),
         vm(HALF, WIDTH),
-        vm(2, shards, *tile),
-        vm(2, shards, *tile),
-        vm(2, shards, *tile),
-        vm(2, RING, (RING - 1) * NZ, *tile),
-        vm(2, RING, NZ, *tile),
-        vm(2, (RING - 1) * NZ, *tile),
-        vm(2, NZ, *tile, dtype=F32),
-        vm(2, NZ, *tile),
-        vm(2, NZ - 1, *tile),
+        vm(count, shards, *tile),
+        vm(count, shards, *tile),
+        vm(count, shards, *tile),
+        vm(count, RING, (RING - 1) * NZ, *tile),
+        vm(count, RING, NZ, *tile),
+        vm(count, (RING - 1) * NZ, *tile),
+        vm(count, NZ, *tile, dtype=F32),
+        vm(count, NZ, *tile),
+        vm(count, NZ - 1, *tile),
     ]
     dma = pltpu.SemaphoreType.DMA
     scratch += [
         dma((6,)),
         dma((2 * CHUNKS,)),
-        dma((5,)),
         dma((1,)),
         dma((1,)),
-        dma((6,)),
-        dma((4 * G_COUNT + 2 * R_COUNT,)),
+        dma((3 * count,)),
+        dma((2 * count * G_COUNT + count * R_COUNT,)),
     ]
     shape = pltpu.VMEM
     outs = pl.pallas_call(

time: 77.9 us -> 71.5 us (0.918)
  Pallas kernels: 77.1 us -> 70.7 us
    pallas_call x1, Pallas kernels: 75 us -> 68.6 us  [body(): pl.pallas_call(step_kernel, out_shape=[shape((HALF, WIDTH), BF16), shape(...]
where the time goes in v4:
time: 71.5 us; the launch traced here: 71.4 us
  Pallas kernels  70.7 us (99%)
    pallas_call x1, Pallas kernels, body(): pl.pallas_call(step_kernel, out_shape=[shape((HALF, WIDTH), BF16), shape(...  68.6 us
    pallas_call x1, Pallas kernels, copied(): pl.pallas_call(functools.partial(copy_kernel, len(arrays)), out_shape=[ja...  2.1 us

profile of v4, /device:TPU:2, one launch (start us, length us, event | category | flops | bytes accessed | tf_op | source)
XLA Modules:
  0.0 71.4 jit_solution(2765197961495858610)
XLA Ops:
  0.6 68.6 %adam_step.1 = (bf16[2048,512]{1,0:T(8,128)(2,1)S(1)}, bf16[16,512]{1,0:T(8,128)(2,1)S(1)}, f32[1,16]{1,0:T(1,128)S(1)}, f32[16,512]{1,0:T(8,128)S(1)}, f32[16,5...) custom-call(bf16[736,4096]{1,0:T(8,128)(2,1)} %act.1, bf16[736,512]{1,0:T(8,128)(2,1)} %grads.1, ...), custom_call_target="tpu_custom_call" | custom-call | flops 3087007744 | bytes 14000000 | tf_op jit(solution)/shard_map/adam_step/pallas_call | solution.py:552
  69.3 2.1 %hand_out.1 = (bf16[2048,512]{1,0:T(8,128)(2,1)}, bf16[16,512]{1,0:T(8,128)(2,1)}, f32[1,16]{1,0:T(1,128)}, f32[16,512]{1,0:T(8,128)}, f32[16,512]{1,0:T(8,128)}, /*index=5*/bf16[2048,512]{1,0:T(8,128)(2,1)}) custom-call(bf16[2048,512]{1,0:T(8,128)(2,1)S(1)} %get-tuple-element.18.refs_0_, bf16[16,512]{1,0:T(8,128)(2,1)S(1)} %get-tuple-element.19.refs_1_, ...), custom_call_target="tpu_custom_call" | custom-call | tf_op jit(solution)/shard_map/hand_out/pallas_call | solution.py:498

commit v5 on v4

--- a/solution.py
+++ b/solution.py
@@ -70,7 +70,7 @@
         pltpu.make_async_copy(like, like, self.send_sems.at[send]).wait()
 
 
-G_FIRST, G_MID, G_ROW, G_COUNT = 0, 0, 4, 8
+G_FIRST, G_MID, G_ROW, G_LEFT, G_RIGHT, G_COUNT = 0, 0, 4, 8, 9, 10
 R_FIRST, R_MID, R_ROW, R_COUNT = 0, 1, 2, 6
 
 
@@ -84,6 +84,9 @@
 
 def unpacked(tile):
     return unpacked_sum(tile.astype(F32))
+
+
+NEAR = (0,)
 
 
 class Gather:
@@ -116,8 +119,33 @@
         for k in (2, 1, 3):
             self.go(block, G_ROW + row, part.dp_pq(part.at_p(k), part.q))
 
+    def halves(self, p, row):
+        q = self.part.at_q(row)
+        return self.part.half(self.buf, p, q, 0), self.part.half(self.buf, p, q, 1)
+
+    def last_near(self, row):
+        part = self.part
+        lower, upper = self.halves(part.p, row)
+        after, before = part.dp_pq(part.at_p(1), part.q), part.dp_pq(part.at_p(-1), part.q)
+        slot = NEAR.index(row)
+        self.go(lower, G_LEFT + slot, after)
+        self.go(upper, G_RIGHT + slot, before)
+        self.go(upper, G_ROW + row, after)
+        self.go(lower, G_ROW + row, before)
+
+    def relay(self, row):
+        part = self.part
+        slot = NEAR.index(row)
+        lower = self.halves(part.at_p(-1), row)[0]
+        part.wait(lower, self.recv + G_LEFT + slot)
+        self.go(lower, G_ROW + row, part.dp_pq(part.at_p(1), part.q))
+        upper = self.halves(part.at_p(1), row)[1]
+        part.wait(upper, self.recv + G_RIGHT + slot)
+        self.go(upper, G_ROW + row, part.dp_pq(part.at_p(-1), part.q))
+
     def row_here(self, row):
-        self.part.wait(self.buf.at[pl.ds(0, 3 * NZ)], self.recv + G_ROW + row)
+        blocks = 3 if row not in NEAR else 2
+        self.part.wait(self.buf.at[pl.ds(0, blocks * NZ)], self.recv + G_ROW + row)
 
     def drain(self):
         self.part.drain(self.buf.at[pl.ds(0, NX * NY * NZ - 1)], self.send_sem)
@@ -126,16 +154,21 @@
 def begin(gathers):
     for g in gathers:
         g.first_here()
+        g.mid()
     for g in gathers:
-        g.mid()
-        g.last(0)
+        g.last_near(0)
 
 
 def spread(gathers):
-    for k in (1, 3, 2):
+    for k in (1, 3):
         for g in gathers:
             g.mid_here(k)
             g.last(RING - k)
+    for g in gathers:
+        g.relay(0)
+    for g in gathers:
+        g.mid_here(2)
+        g.last(2)
 
 
 def here(gathers, rows):
@@ -337,14 +370,12 @@
             rows = chunk_rows(k)
             own_g[rows] = product(k + CHUNKS) * factor + werr_v[rows].astype(F32)
 
+    begin(gathers)
     load_werr.wait()
-    for_own(0, 4)
-
-    for gs in by_group(gathers):
-        begin(gs)
-    for_own(4, 8)
+    for_own(0, 6)
     for gs in by_group(gathers):
         spread(gs)
+    for_own(6, 8)
     pltpu.make_async_copy(peer_rx, peer_rx, peer_recv.at[0]).wait()
 
     @pl.loop(0, HALF // 64)
@@ -413,11 +444,6 @@
                     r.last(row, 1)
                     r.last(row, 3)
 
-    @pl.loop(0, HALF // 64)
-    def _(t):
-        rows = pl.ds(pl.multiple_of(t * 64, 64), 64)
-        left_out[rows] = left_v[rows].astype(BF16)
-
     for rs in by_group(reduces):
 
         @pl.loop(0, RING - 1)
@@ -431,6 +457,7 @@
     for rs in by_group(reduces):
         for r in rs:
             r.first(dp_z)
+
     load_serr.wait()
     load_master.wait()
     load_variance.wait()
@@ -464,6 +491,11 @@
         jnp.where(eye, jnp.broadcast_to(scale, (OWN, OWN)), 0.0), axis=0, keepdims=True
     )
 
+    @pl.loop(0, HALF // 64)
+    def _(t):
+        rows = pl.ds(pl.multiple_of(t * 64, 64), 64)
+        left_out[rows] = left_v[rows].astype(BF16)
+
     def assemble(yy, xx, at):
         for zz in range(NZ):
             for i in range(2):
@@ -472,8 +504,7 @@
                     rows, axis=0
                 ).astype(BF16)
 
-    for gs in by_group(gathers_w):
-        begin(gs)
+    begin(gathers_w)
     for gs in by_group(gathers_w):
         spread(gs)
     here(gathers_w, near_rows)

time: 71.5 us -> 69.5 us (0.972)
  Pallas kernels: 70.7 us -> 68.7 us
    pallas_call x1, Pallas kernels: 68.6 us -> 66.6 us  [body(): pl.pallas_call(step_kernel, out_shape=[shape((HALF, WIDTH), BF16), shape(...]
where the time goes in v5:
time: 69.5 us; the launch traced here: 69.4 us
  Pallas kernels  68.7 us (99%)
    pallas_call x1, Pallas kernels, body(): pl.pallas_call(step_kernel, out_shape=[shape((HALF, WIDTH), BF16), shape(...  66.6 us
    pallas_call x1, Pallas kernels, copied(): pl.pallas_call(functools.partial(copy_kernel, len(arrays)), out_shape=[ja...  2.1 us

profile of v5, /device:TPU:2, one launch (start us, length us, event | category | flops | bytes accessed | tf_op | source)
XLA Modules:
  0.0 69.4 jit_solution(4945546520169923191)
XLA Ops:
  0.6 66.6 %adam_step.1 = (bf16[2048,512]{1,0:T(8,128)(2,1)S(1)}, bf16[16,512]{1,0:T(8,128)(2,1)S(1)}, f32[1,16]{1,0:T(1,128)S(1)}, f32[16,512]{1,0:T(8,128)S(1)}, f32[16,5...) custom-call(bf16[736,4096]{1,0:T(8,128)(2,1)} %act.1, bf16[736,512]{1,0:T(8,128)(2,1)} %grads.1, ...), custom_call_target="tpu_custom_call" | custom-call | flops 3087007744 | bytes 14000000 | tf_op jit(solution)/shard_map/adam_step/pallas_call | solution.py:583
  67.3 2.1 %hand_out.1 = (bf16[2048,512]{1,0:T(8,128)(2,1)}, bf16[16,512]{1,0:T(8,128)(2,1)}, f32[1,16]{1,0:T(1,128)}, f32[16,512]{1,0:T(8,128)}, f32[16,512]{1,0:T(8,128)}, /*index=5*/bf16[2048,512]{1,0:T(8,128)(2,1)}) custom-call(bf16[2048,512]{1,0:T(8,128)(2,1)S(1)} %get-tuple-element.18.refs_0_, bf16[16,512]{1,0:T(8,128)(2,1)S(1)} %get-tuple-element.19.refs_1_, ...), custom_call_target="tpu_custom_call" | custom-call | tf_op jit(solution)/shard_map/hand_out/pallas_call | solution.py:529

commit v6 on v5

--- a/solution.py
+++ b/solution.py
@@ -496,21 +496,25 @@
         rows = pl.ds(pl.multiple_of(t * 64, 64), 64)
         left_out[rows] = left_v[rows].astype(BF16)
 
-    def assemble(yy, xx, at):
-        for zz in range(NZ):
+    def assemble(row):
+        @pl.loop(0, RING)
+        def _(p):
             for i in range(2):
-                rows = [unpacked(wts[2 * group + i, at[i] + zz]) for group in range(GROUPS)]
-                weights_out[zz, yy, xx, :, parts[i].columns] = jnp.concatenate(
-                    rows, axis=0
-                ).astype(BF16)
+                q = parts[i].at_q(row)
+                xx, yy = (p, q) if i == 0 else (q, p)
+                for zz in range(NZ):
+                    at = (p * RING + q) * NZ + zz
+                    rows = [unpacked(wts[2 * group + i, at]) for group in range(GROUPS)]
+                    weights_out[zz, yy, xx, :, parts[i].columns] = jnp.concatenate(
+                        rows, axis=0
+                    ).astype(BF16)
 
     begin(gathers_w)
     for gs in by_group(gathers_w):
         spread(gs)
-    here(gathers_w, near_rows)
-    near_blocks(assemble)
-    here(gathers_w, (2,))
-    far_blocks(assemble)
+    for row in (*near_rows, 2):
+        here(gathers_w, (row,))
+        assemble(row)
     for g in gathers + gathers_w + reduces:
         g.drain()
     pltpu.make_async_copy(peer_tx, peer_tx, peer_send.at[0]).wait()

time: 69.5 us -> 69.4 us (level)
  no operation moved by 1% of the time
where the time goes in v6:
time: 69.4 us; the launch traced here: 69.3 us
  Pallas kernels  68.6 us (99%)
    pallas_call x1, Pallas kernels, body(): pl.pallas_call(step_kernel, out_shape=[shape((HALF, WIDTH), BF16), shape(...  66.5 us
    pallas_call x1, Pallas kernels, copied(): pl.pallas_call(functools.partial(copy_kernel, len(arrays)), out_shape=[ja...  2.1 us

profile of v6, /device:TPU:2, one launch (start us, length us, event | category | flops | bytes accessed | tf_op | source)
XLA Modules:
  0.0 69.3 jit_solution(8028234446740056569)
XLA Ops:
  0.6 66.5 %adam_step.1 = (bf16[2048,512]{1,0:T(8,128)(2,1)S(1)}, bf16[16,512]{1,0:T(8,128)(2,1)S(1)}, f32[1,16]{1,0:T(1,128)S(1)}, f32[16,512]{1,0:T(8,128)S(1)}, f32[16,5...) custom-call(bf16[736,4096]{1,0:T(8,128)(2,1)} %act.1, bf16[736,512]{1,0:T(8,128)(2,1)} %grads.1, ...), custom_call_target="tpu_custom_call" | custom-call | flops 3087007744 | bytes 14000000 | tf_op jit(solution)/shard_map/adam_step/pallas_call | solution.py:587
  67.2 2.1 %hand_out.1 = (bf16[2048,512]{1,0:T(8,128)(2,1)}, bf16[16,512]{1,0:T(8,128)(2,1)}, f32[1,16]{1,0:T(1,128)}, f32[16,512]{1,0:T(8,128)}, f32[16,512]{1,0:T(8,128)}, /*index=5*/bf16[2048,512]{1,0:T(8,128)(2,1)}) custom-call(bf16[2048,512]{1,0:T(8,128)(2,1)S(1)} %get-tuple-element.18.refs_0_, bf16[16,512]{1,0:T(8,128)(2,1)S(1)} %get-tuple-element.19.refs_1_, ...), custom_call_target="tpu_custom_call" | custom-call | tf_op jit(solution)/shard_map/hand_out/pallas_call | solution.py:533
